TPU v7x, 256 devices: a whole 4x4x8 slice. The times are simulated.
256 devices in a mesh: dp: 8 (over y, x_hi), expert: 16 (over x_lo, z), tensor: 2 (over core).
Axes of the slice: x: 4 (x_hi: 2, x_lo: 2; x = x_hi * 2 + x_lo), y: 4, z: 8, core: 2. Of those that a mesh axis runs over, the one named last changes fastest.
Arguments:
- tokens: bfloat16 [16384, 4096], P(('dp', 'expert'), 'tensor'), may hold values from -6 to 6
- routes: int32 [16384, 2], P(('dp', 'expert')), may hold values from 0 to 14, as said below
- gates: float32 [16384, 2], P(('dp', 'expert')), may hold values from 0.2 to 1
- dropped: int32 [16384, 2], P(('dp', 'expert')), may hold values from 0 to 1, as said below
- placement: int32 [15], replicated, may hold values from 0 to 15, as said below
- w_gate: bfloat16 [16, 4096, 768], P('expert', None, 'tensor'), may hold values from -0.09375 to 0.09375
- w_up: bfloat16 [16, 4096, 768], P('expert', None, 'tensor'), may hold values from -0.09375 to 0.09375
- w_down: bfloat16 [16, 768, 4096], P('expert', 'tensor'), may hold values from -0.21875 to 0.21875
- cotangent: bfloat16 [16384, 4096], P(('dp', 'expert'), 'tensor'), may hold values from -1.1953125 to 1.1953125
Outputs:
- mixed: bfloat16 [16384, 4096], P(('dp', 'expert'), 'tensor')
- input_grad: bfloat16 [16384, 4096], P(('dp', 'expert'), 'tensor')
- grad_gate: bfloat16 [16, 4096, 768], P('expert', 'dp', 'tensor')
- grad_up: bfloat16 [16, 4096, 768], P('expert', 'dp', 'tensor')
- grad_down: bfloat16 [16, 768, 4096], P('expert', 'tensor', 'dp')
Inputs may be any that keep to these rules, and one draw needn't show every extreme that they name: `routes`: each token names 2 different experts below 15; one expert, the same in every block, is named by every token. `dropped`: within an aligned block of 128 tokens every expert keeps at most 32 routes, and the expert named by every token keeps exactly 32 in every block. `placement`: 15 distinct slots below 16; one slot, neither the first nor the last, hosts no expert.
All inputs are finite; a program needn't handle non-finite values.
Results may differ from a plain program's by a relative error of at most 0.017.
Values may be sent and summed in bfloat16 or wider, within the bound.
A program may use at most 192 MiB of HBM per device.

v0:
```python
import jax
import jax.numpy as jnp
from jax import lax
from jax.sharding import PartitionSpec as P


def route_targets(routes, dropped, placement, capacity):
    route_total = routes.shape[0] * routes.shape[1]
    labels = jnp.arange(placement.shape[0], dtype=jnp.int32)
    flat_routes = routes.reshape(route_total)
    kept_mask = dropped.reshape(route_total) == 0
    hit_table = jnp.where(
        (flat_routes[:, None] == labels[None, :]) & kept_mask[:, None], 1, 0
    ).astype(jnp.int32)
    before = jnp.cumsum(hit_table, axis=0) - hit_table
    position = jnp.sum(before * hit_table, axis=1)
    target = jnp.sum(hit_table * placement[None, :], axis=1)
    return (jnp.where(kept_mask, target * capacity + position, -1), kept_mask)


def route_matrix(buffer_row, weights, buffer_count, route_count):
    token_count = buffer_row.shape[0] // route_count
    row_ids = jnp.arange(buffer_count, dtype=jnp.int32)
    matched = buffer_row.reshape(token_count, route_count)[None, :, :] == row_ids[:, None, None]
    spread = jnp.where(matched, weights.reshape(token_count, route_count)[None, :, :], 0.0)
    return jnp.sum(spread, axis=2)


def gather_routes(returned, buffer_row, weights, route_count):
    features = returned.shape[2]
    flat_back = returned.reshape(-1, features)
    picked = jnp.take(flat_back, jnp.maximum(buffer_row, 0), axis=0).astype(jnp.float32)
    scaled = picked * weights[:, None]
    return jnp.sum(scaled.reshape(-1, route_count, features), axis=1)


def per_device(tokens, routes, gates, dropped, placement, w_gate, w_up, w_down, cotangent):
    token_count = tokens.shape[0]
    route_count = routes.shape[1]
    expert_count = placement.shape[0]
    slot_count = lax.axis_size("expert")
    capacity = min(
        token_count,
        (3 * token_count * route_count + 16 * expert_count - 1) // (16 * expert_count) * 8,
    )
    buffer_count = slot_count * capacity
    buffer_row, kept_mask = route_targets(routes, dropped, placement, capacity)
    route_gate = jnp.where(kept_mask, gates.reshape(-1), 0.0)
    kept_weight = jnp.where(kept_mask, 1.0, 0.0).astype(jnp.float32)
    select_plain = route_matrix(buffer_row, kept_weight, buffer_count, route_count).astype(
        jnp.bfloat16
    )
    token_send = jnp.dot(select_plain, tokens, preferred_element_type=jnp.float32).astype(
        jnp.bfloat16
    )
    token_send = token_send.reshape(slot_count, capacity, -1)
    row_gate = jnp.sum(route_matrix(buffer_row, route_gate, buffer_count, route_count), axis=1)
    grad_picked = jnp.dot(select_plain, cotangent, preferred_element_type=jnp.float32)
    grad_send = (
        (grad_picked * row_gate[:, None]).astype(jnp.bfloat16).reshape(slot_count, capacity, -1)
    )
    got_tokens = lax.all_to_all(token_send, "expert", split_axis=0, concat_axis=0, tiled=True)
    expert_rows = lax.all_gather(got_tokens, "tensor", axis=2, tiled=True)
    features = expert_rows.shape[2]
    expert_rows = expert_rows.reshape(buffer_count, features)
    gate_matrix = w_gate[0]
    up_matrix = w_up[0]
    down_matrix = w_down[0]
    ff_dev = gate_matrix.shape[1]
    gate_pre = jnp.dot(expert_rows, gate_matrix, preferred_element_type=jnp.float32)
    up_pre = jnp.dot(expert_rows, up_matrix, preferred_element_type=jnp.float32)
    sigmoid_gate = jax.nn.sigmoid(gate_pre)
    silu_gate = gate_pre * sigmoid_gate
    hidden = (silu_gate * up_pre).astype(jnp.bfloat16)
    out_part = jnp.dot(hidden, down_matrix, preferred_element_type=jnp.float32).reshape(
        slot_count, capacity, features
    )
    out_half = lax.psum_scatter(
        out_part.astype(jnp.bfloat16), "tensor", scatter_dimension=2, tiled=True
    )
    out_back = lax.all_to_all(out_half, "expert", split_axis=0, concat_axis=0, tiled=True)
    got_grads = lax.all_to_all(grad_send, "expert", split_axis=0, concat_axis=0, tiled=True)
    grad_in = lax.all_gather(got_grads, "tensor", axis=2, tiled=True)
    grad_in = grad_in.reshape(buffer_count, features)
    contract = (((1,), (1,)), ((), ()))
    grad_hidden = lax.dot_general(
        grad_in, down_matrix, contract, preferred_element_type=jnp.float32
    )
    slope = sigmoid_gate * (1.0 + gate_pre * (1.0 - sigmoid_gate))
    grad_gate_pre = (grad_hidden * up_pre * slope).astype(jnp.bfloat16)
    grad_up_pre = (grad_hidden * silu_gate).astype(jnp.bfloat16)
    input_part = lax.dot_general(
        grad_gate_pre, gate_matrix, contract, preferred_element_type=jnp.float32
    )
    input_part = input_part + lax.dot_general(
        grad_up_pre, up_matrix, contract, preferred_element_type=jnp.float32
    )
    input_part = input_part.reshape(slot_count, capacity, features)
    input_half = lax.psum_scatter(
        input_part.astype(jnp.bfloat16), "tensor", scatter_dimension=2, tiled=True
    )
    input_back = lax.all_to_all(input_half, "expert", split_axis=0, concat_axis=0, tiled=True)
    mixed = gather_routes(out_back, buffer_row, route_gate, route_count).astype(jnp.bfloat16)
    input_grad = gather_routes(input_back, buffer_row, kept_weight, route_count).astype(
        jnp.bfloat16
    )
    along_rows = (((0,), (0,)), ((), ()))
    gate_term = lax.dot_general(
        expert_rows, grad_gate_pre, along_rows, preferred_element_type=jnp.float32
    )
    up_term = lax.dot_general(
        expert_rows, grad_up_pre, along_rows, preferred_element_type=jnp.float32
    )
    down_term = lax.dot_general(grad_in, hidden, along_rows, preferred_element_type=jnp.float32)
    summed = lax.psum_scatter(
        jnp.concatenate([gate_term, up_term, down_term], axis=1).astype(jnp.bfloat16),
        "dp",
        scatter_dimension=0,
        tiled=True,
    ).astype(jnp.float32)
    grad_gate = summed[:, :ff_dev]
    grad_up = summed[:, ff_dev : 2 * ff_dev]
    grad_down = summed[:, 2 * ff_dev :].T
    return (
        mixed,
        input_grad,
        grad_gate.astype(jnp.bfloat16)[None],
        grad_up.astype(jnp.bfloat16)[None],
        grad_down.astype(jnp.bfloat16)[None],
    )


def solution(mesh):
    in_specs = (
        P(("dp", "expert"), "tensor"),
        P(("dp", "expert"), None),
        P(("dp", "expert"), None),
        P(("dp", "expert"), None),
        P(),
        P("expert", None, "tensor"),
        P("expert", None, "tensor"),
        P("expert", "tensor", None),
        P(("dp", "expert"), "tensor"),
    )
    out_specs = (
        P(("dp", "expert"), "tensor"),
        P(("dp", "expert"), "tensor"),
        P("expert", "dp", "tensor"),
        P("expert", "dp", "tensor"),
        P("expert", "tensor", "dp"),
    )
    return jax.shard_map(
        per_device, mesh=mesh, in_specs=in_specs, out_specs=out_specs, check_vma=False
    )
```

profile of v0, /device:TPU:1, one launch (start us, length us, event | category | flops | bytes accessed | tf_op | source)
XLA Modules:
  0.0 374.0 jit_solution(18329450126364129983)
XLA Ops:
  7.2 0.9 copy.28
  12.6 1.7 convolution_convert_fusion.4
  14.4 57.4 %all_to_all.20 = bf16[16,32,2048]{2,1,0:T(8,128)(2,1)} all-to-all(bf16[16,32,2048]{2,1,0:T(8,128)(2,1)S(1)} %bitcast.58), channel_id=1, replica_groups=mesh['dp'=8,'expert'=16,'tensor'=2] {'expert'}, dimensions={0} | all-to-all | bytes 4194304 | tf_op jit(solution)/shard_map/all_to_all | solution.py:62
  71.8 1.7 multiply_convert_fusion
  73.6 52.5 %all_to_all.21 = bf16[16,32,2048]{2,1,0:T(8,128)(2,1)} all-to-all(bf16[16,32,2048]{2,1,0:T(8,128)(2,1)S(1)} %bitcast.57), channel_id=1, replica_groups=mesh['dp'=8,'expert'=16,'tensor'=2] {'expert'}, dimensions={0} | all-to-all | bytes 4194304 | tf_op jit(solution)/shard_map/all_to_all | solution.py:82
  126.2 6.5 %fusion.4 = f32[512,384]{1,0:T(8,128)} fusion(bf16[512,4096]{1,0:T(8,128)(2,1)} %bitcast.61, bf16[1,4096,384]{2,1,0:T(8,128)(2,1)} %param.17), kind=kOutput, calls=%fused_computation.13 | convolution fusion | flops 1610612736 | bytes 8126464 | tf_op jit(solution)/shard_map/dot_general | solution.py:71
  132.7 3.2 fusion.8
  135.9 11.2 %all-gather.5.cloned.1.call-done = bf16[16,32,4096]{2,1,0:T(8,128)(2,1)} async-done(((bf16[16,32,2048]{2,1,0:T(8,128)(2,1)}), bf16[16,32,4096]{2,1,0:T(8,128)(2,1)}) %all-gather.5.cloned.1.call-update) | async-done | bytes 4194320 | tf_op jit(solution)/shard_map/all_gather | solution.py:83
  147.1 6.0 %multiply_convert_fusion.1 = (bf16[512,384]{1,0:T(8,128)(2,1)}, bf16[512,384]{1,0:T(8,128)(2,1)}, bf16[512,384]{1,0:T(8,128)(2,1)S(1)}) fusion(f32[512,384]{1,0:T(8,128)} %fusion.8, f32[512,384]{1,0:T(8,128)} %fusion.4, bf16[512,4096]{1,0:T(8,128)(2,1)} %bitcast.65, bf16[1,384,4096]{2,1,0:T(8,128)(2,1)S(1)} %copy-done), kind=kOutput, calls=%fused_computation.22 | convolution fusion | flops 1613561856 | bytes 10092544 | tf_op jit(solution)/shard_map/dot_general | solution.py:86
  153.8 4.4 %convolution_convert_fusion = bf16[16,32,4096]{2,1,0:T(8,128)(2,1)} fusion(bf16[16,32,384]{2,1,0:T(8,128)(2,1)S(1)} %bitcast.67, bf16[1,384,4096]{2,1,0:T(8,128)(2,1)S(1)} %copy-done), kind=kOutput, calls=%fused_computation.4 | convolution fusion | flops 1612709888 | bytes 7733248 | tf_op jit(solution)/shard_map/dot_general | solution.py:75
  158.5 1.6 copy-done.3
  160.1 3.5 fusion.6
  163.7 4.3 %add_convert_fusion = bf16[512,4096]{1,0:T(8,128)(2,1)} fusion(f32[512,4096]{1,0:T(8,128)S(1)} %fusion.6, bf16[512,384]{1,0:T(8,128)(2,1)S(1)} %copy-done.6, bf16[1,4096,384]{2,1,0:T(8,128)(2,1)S(1)} %copy-done.4), kind=kOutput, calls=%fused_computation.3 | convolution fusion | flops 1614807040 | bytes 16121856 | tf_op jit(solution)/shard_map/dot_general | solution.py:95
  168.1 4.4 %convolution_convert_fusion.1 = bf16[4096,384]{0,1:T(8,128)(2,1)S(1)} fusion(bf16[512,4096]{1,0:T(8,128)(2,1)} %bitcast.66, bf16[512,384]{1,0:T(8,128)(2,1)} %copy-done.10), kind=kOutput, calls=%fused_computation.5 | convolution fusion | flops 1612185600 | bytes 7733248 | tf_op jit(solution)/shard_map/dot_general | solution.py:114
  172.5 1.9 convolution_convert_fusion.2
  174.4 1.9 convolution_convert_fusion.3
  176.3 4.4 %pad_maximum_fusion = bf16[4096,1152]{0,1:T(8,128)(2,1)} fusion(bf16[4096,384]{0,1:T(8,128)(2,1)S(1)} %convolution_convert_fusion.1, bf16[4096,384]{0,1:T(8,128)(2,1)S(1)} %convolution_convert_fusion.2, bf16[4096,384]{0,1:T(8,128)(2,1)S(1)} %convolution_convert_fusion.3), kind=kLoop, calls=%fused_computation.2 | loop fusion | flops 28311552 | bytes 18874368 | tf_op jit(solution)/shard_map/concatenate | solution.py:116
  180.7 7.4 %all-to-all-start.1 = ((bf16[16,32,2048]{2,1,0:T(8,128)(2,1)}), bf16[16,32,2048]{2,1,0:T(8,128)(2,1)S(1)}, u32[]{:S(2)}, u32[]{:S(2)}) async-start(bf16[16,32,2048]{2,1,0:T(8,128)(2,1)} %reduce-scatter.4.cloned.1.call-done), calls=%async_computation.2 | async-start | bytes 4194304 | tf_op jit(solution)/shard_map/all_to_all | solution.py:81
  188.1 10.2 %reduce-scatter.6.cloned.1.call-done = bf16[16,32,2048]{2,1,0:T(8,128)(2,1)} async-done(((bf16[16,32,4096]{2,1,0:T(8,128)(2,1)}), bf16[16,32,2048]{2,1,0:T(8,128)(2,1)}) %reduce-scatter.6.cloned.1.call-update) | async-done | bytes 2097168 | tf_op jit(solution)/shard_map/reduce_scatter | solution.py:99
  198.3 38.4 %all-to-all-done.1 = bf16[16,32,2048]{2,1,0:T(8,128)(2,1)S(1)} async-done(((bf16[16,32,2048]{2,1,0:T(8,128)(2,1)}), bf16[16,32,2048]{2,1,0:T(8,128)(2,1)S(1)}, u32[]{:S(2)}, u32[]{:S(2)}) %all-to-all-start.1) | async-done | bytes 2097184 | tf_op jit(solution)/shard_map/all_to_all | solution.py:81
  236.7 6.6 %all-to-all-start.3 = ((bf16[16,32,2048]{2,1,0:T(8,128)(2,1)}), bf16[16,32,2048]{2,1,0:T(8,128)(2,1)}, u32[]{:S(2)}, u32[]{:S(2)}) async-start(bf16[16,32,2048]{2,1,0:T(8,128)(2,1)} %reduce-scatter.6.cloned.1.call-done), calls=%async_computation.5 | async-start | bytes 4194304 | tf_op jit(solution)/shard_map/all_to_all | solution.py:102
  243.4 1.4 gather_fusion
  244.8 46.8 %all-to-all-done.3 = bf16[16,32,2048]{2,1,0:T(8,128)(2,1)} async-done(((bf16[16,32,2048]{2,1,0:T(8,128)(2,1)}), bf16[16,32,2048]{2,1,0:T(8,128)(2,1)}, u32[]{:S(2)}, u32[]{:S(2)}) %all-to-all-start.3) | async-done | bytes 2097184 | tf_op jit(solution)/shard_map/all_to_all | solution.py:102
  291.6 5.2 %gather_fusion.1 = bf16[256,2048]{1,0:T(8,128)(2,1)} fusion(bf16[512,2048]{1,0:T(8,128)(2,1)} %bitcast.12, s32[1024]{0:T(1024)S(1)} %pad_clamp_fusion), kind=kCustom, calls=%fused_computation.1.clone | custom fusion | bytes 2098176 | tf_op jit(solution)/shard_map/jit(_take)/gather | solution.py:32
  296.8 3.0 convert_multiply_fusion
  299.8 3.6 reshape.124
  303.3 2.2 reshape.120
  305.5 5.1 %reduce_sum.63 = bf16[128,2048]{1,0:T(8,128)(2,1)} reduce(f32[128,2,2048]{2,1,0:T(2,128)} %reshape.124, f32[]{:T(128)} %constant.5.clone.1), dimensions={1}, to_apply=%region_9.11 | reduce | flops 262144 | bytes 2621444 | tf_op jit(solution)/shard_map/reduce_sum | solution.py:34
  310.7 5.1 %reduce_sum.61 = bf16[128,2048]{1,0:T(8,128)(2,1)} reduce(f32[128,2,2048]{2,1,0:T(2,128)} %reshape.120, f32[]{:T(128)} %constant.5.clone.1), dimensions={1}, to_apply=%region_6.8 | reduce | flops 262144 | bytes 2621444 | tf_op jit(solution)/shard_map/reduce_sum | solution.py:34
  315.7 46.7 %reduce-scatter.8.cloned.1.call-done = bf16[512,1152]{0,1:T(8,128)(2,1)} async-done(((bf16[4096,1152]{0,1:T(8,128)(2,1)}), bf16[512,1152]{0,1:T(8,128)(2,1)}) %reduce-scatter.8.cloned.1.call-update) | async-done | bytes 1179664 | tf_op jit(solution)/shard_map/reduce_scatter | solution.py:115
  362.4 2.2 slice_bitcast_fusion
  364.6 1.9 copy.37
  (62 shorter events, 6.8 us)
Async XLA Ops:
  7.2 139.9 %copy-start = (bf16[1,384,4096]{2,1,0:T(8,128)(2,1)S(1)}, bf16[1,384,4096]{2,1,0:T(8,128)(2,1)}, u32[]{:S(2)}) copy-start(bf16[1,384,4096]{2,1,0:T(8,128)(2,1)} %param.18) | copy-start | bytes 9437188
  7.2 119.0 %all-gather.3.cloned.1.call-start = ((), (), s32[]{:S(2)}) async-start(), calls=%async_computation.7 | async-start | bytes 6291456 | tf_op jit(solution)/shard_map/all_gather | solution.py:63
  71.8 75.3 %all-gather.5.cloned.1.call-start = ((), (), s32[]{:S(2)}) async-start(), calls=%async_computation.9 | async-start | bytes 6291456 | tf_op jit(solution)/shard_map/all_gather | solution.py:83
  126.1 54.6 %reduce-scatter.4.cloned.1.call-start = ((), (), s32[]{:S(2)}) async-start(), calls=%async_computation.8 | async-start | bytes 6291456 | tf_op jit(solution)/shard_map/reduce_scatter | solution.py:78
  126.2 6.5 %copy-start.2 = (bf16[1,4096,384]{2,1,0:T(8,128)(2,1)S(1)}, bf16[1,4096,384]{2,1,0:T(8,128)(2,1)}, u32[]{:S(2)}) copy-start(bf16[1,4096,384]{2,1,0:T(8,128)(2,1)} %param.16) | copy-start | bytes 9437188
  126.2 6.5 %copy-start.8 = (bf16[16,32,4096]{2,1,0:T(8,128)(2,1)S(1)}, bf16[16,32,4096]{2,1,0:T(8,128)(2,1)}, u32[]{:S(2)}) copy-start(bf16[16,32,4096]{2,1,0:T(8,128)(2,1)} %all-gather.3.cloned.1.call-done) | copy-start | bytes 12582916
  153.1 0.7 copy-start.10
  158.2 1.9 copy-start.3
  158.3 40.0 %reduce-scatter.6.cloned.1.call-start = ((), (), s32[]{:S(2)}) async-start(), calls=%async_computation.10 | async-start | bytes 6291456 | tf_op jit(solution)/shard_map/reduce_scatter | solution.py:99
  160.1 3.5 copy-start.4
  160.1 3.5 copy-start.6
  168.0 194.4 %reduce-scatter.8.cloned.1.call-start = ((), (), s32[]{:S(2)}) async-start(), calls=%async_computation.11 | async-start | bytes 10616832 | tf_op jit(solution)/shard_map/reduce_scatter | solution.py:115
  168.1 4.4 %copy-start.7 = (bf16[512,384]{1,0:T(8,128)(2,1)S(1)}, bf16[512,384]{1,0:T(8,128)(2,1)}, u32[]{:S(2)}) copy-start(bf16[512,384]{1,0:T(8,128)(2,1)} %get-tuple-element.30) | copy-start | bytes 1179652
  168.1 4.4 %copy-start.9 = (bf16[16,32,4096]{2,1,0:T(8,128)(2,1)S(1)}, bf16[16,32,4096]{2,1,0:T(8,128)(2,1)}, u32[]{:S(2)}) copy-start(bf16[16,32,4096]{2,1,0:T(8,128)(2,1)} %all-gather.3.cloned.1.call-done) | copy-start | bytes 12582916
  172.5 1.9 copy-start.5
  180.7 56.0 %all-to-all-start.1 = ((bf16[16,32,2048]{2,1,0:T(8,128)(2,1)}), bf16[16,32,2048]{2,1,0:T(8,128)(2,1)S(1)}, u32[]{:S(2)}, u32[]{:S(2)}) async-start(bf16[16,32,2048]{2,1,0:T(8,128)(2,1)} %reduce-scatter.4.cloned.1.call-done), calls=%async_computation.2 | async-start | bytes 4194304 | tf_op jit(solution)/shard_map/all_to_all | solution.py:81
  236.7 54.9 %all-to-all-start.3 = ((bf16[16,32,2048]{2,1,0:T(8,128)(2,1)}), bf16[16,32,2048]{2,1,0:T(8,128)(2,1)}, u32[]{:S(2)}, u32[]{:S(2)}) async-start(bf16[16,32,2048]{2,1,0:T(8,128)(2,1)} %reduce-scatter.6.cloned.1.call-done), calls=%async_computation.5 | async-start | bytes 4194304 | tf_op jit(solution)/shard_map/all_to_all | solution.py:102
  305.5 61.9 %copy-start.1 = (bf16[1,384,4096]{2,1,0:T(8,128)(2,1)S(1)}, bf16[1,384,4096]{2,1,0:T(8,128)(2,1)}, u32[]{:S(2)}) copy-start(bf16[1,384,4096]{2,1,0:T(8,128)(2,1)} %param.18) | copy-start | bytes 9437188
Sparse Core Ops, SparseCore 0:
  71.9 20.2 all-gather.2
  126.2 20.8 all-gather.4
  158.4 18.4 reduce-scatter.3
  179.5 18.7 reduce-scatter.5
  202.3 160.0 reduce-scatter.7
where the time goes:
time: 375 us; the launch traced here: 374 us
  waiting for transfers between devices  153 us (41%)
  blocking collectives  110 us (29%)
  matrix products  39.6 us (11%)
  local copies, waits for them, and re-layouts  23.5 us (6%)
  other arithmetic  19.3 us (5%)
  starting transfers between devices  14.4 us (4%)
  between operations  14 us (4%)
    all_to_all x1, blocking collectives, per_device(): lax.all_to_all(token_send, 'expert', split_axis=0, concat_axis=0, tiled=T...  57.4 us
    all_to_all x1, blocking collectives, per_device(): lax.all_to_all(grad_send, 'expert', split_axis=0, concat_axis=0, tiled=True)  52.5 us
    all_to_all x1, waiting for transfers between devices, per_device(): lax.all_to_all(input_half, 'expert', split_axis=0, concat_axis=0, tiled=T...  46.8 us
    reduce_scatter x1, waiting for transfers between devices, per_device(): lax.psum_scatter(jnp.concatenate([gate_term, up_term, down_term], axis=1)...  46.7 us
    all_to_all x1, waiting for transfers between devices, per_device(): lax.all_to_all(out_half, 'expert', split_axis=0, concat_axis=0, tiled=True)  38.4 us
    all_gather x1, waiting for transfers between devices, per_device(): grad_in = lax.all_gather(got_grads, 'tensor', axis=2, tiled=True)  11.2 us
    reduce_sum x2, other arithmetic, gather_routes(): return jnp.sum(scaled.reshape(-1, route_count, features), axis=1)  10.2 us
    reduce_scatter x1, waiting for transfers between devices, per_device(): lax.psum_scatter(input_part.astype(jnp.bfloat16), 'tensor', scatter_dimen...  10.2 us
  transfers between devices with their start and end apart: 7, of which 5 were waited for; matrix products, arithmetic and copies ran while one was open for 15% of the time, Pallas kernels for 0%

commit v1 on v0

v1 whole, which is shorter than its diff:
```python
import jax
import jax.numpy as jnp
from jax import lax
from jax.experimental import pallas as pl
from jax.experimental.pallas import tpu as pltpu
from jax.sharding import PartitionSpec as P

MESH = pl.DeviceIdType.MESH
BF = jnp.bfloat16
F32 = jnp.float32
TOK = 128
CAP = 32
ROWS = 16 * CAP
FULL = 4096
HALF = 2048
FF = 384
COL = 512
MIB = 1 << 20

STEPS = ((0, 0), (1, 1), (1, -1), (2, 1), (2, -1))
FAR = {(1, 0): 10, (1, 1): 11, (-1, 0): 12, (-1, 1): 13, (1, 2): 14, (-1, 2): 15}


class Place:
    def __init__(self):
        self.dp = lax.axis_index("dp")
        expert = lax.axis_index("expert")
        self.core = lax.axis_index("tensor")
        self.y = lax.div(self.dp, 2)
        self.xh = lax.rem(self.dp, 2)
        self.x = lax.div(expert, 8)
        self.z = lax.rem(expert, 8)

    def slot(self, dx, dz):
        return lax.rem(self.x + dx, 2) * 8 + lax.rem(self.z + dz + 8, 8)

    def near(self, dx, dz):
        return (self.dp, self.slot(dx, dz), self.core)

    def other_core(self):
        return (self.dp, self.slot(0, 0), 1 - self.core)

    def along_y(self, dy):
        return (lax.rem(self.y + dy + 4, 4) * 2 + self.xh, self.slot(0, 0), self.core)

    def other_xh(self):
        return (self.y * 2 + 1 - self.xh, self.slot(0, 0), self.core)


def barrier(peers):
    sem = pltpu.get_barrier_semaphore()
    for peer in peers:
        pl.semaphore_signal(sem, inc=1, device_id=peer, device_id_type=MESH)
    pl.semaphore_wait(sem, len(peers))


def tree_peers(here):
    return [
        here.near(0, 1), here.near(0, -1), here.near(0, 2), here.near(0, -2), here.near(1, 0),
        here.near(1, 1), here.near(1, -1), here.near(1, 2), here.near(1, -2), here.other_core(),
    ]


def remote(src, dst, send, recv, peer):
    return pltpu.make_async_remote_copy(
        src_ref=src, dst_ref=dst, send_sem=send, recv_sem=recv, device_id=peer, device_id_type=MESH
    )


def slots_of(here, index):
    slots = [here.slot(0, 0), here.slot(1, 0)]
    depth, way = STEPS[index]
    if depth == 2:
        slots += [here.slot(0, way), here.slot(1, way)]
        slots.append(here.slot(0, 2) if way == 1 else here.slot(1, -2))
    return slots


def far_places(index):
    way = STEPS[index][1]
    return [FAR[(way, n)] for n in range(3)]


def far_peer(here, way, n, sign):
    if n == 0:
        return here.near(0, way * sign)
    if n == 1:
        return here.near(1, way * sign)
    return here.near(0, 2 * sign) if way == 1 else here.near(1, -2 * sign)


def hits(meta, slots):
    ids = jnp.concatenate(
        [(s * CAP + lax.broadcasted_iota(jnp.int32, (CAP, TOK), 0)).astype(F32) for s in slots], axis=0
    )
    return meta[0:1, :] == ids, meta[1:2, :] == ids


def plain_table(meta, slots):
    first, second = hits(meta, slots)
    return jnp.where(first | second, 1.0, 0.0).astype(F32)


def gate_table(meta, slots):
    first, second = hits(meta, slots)
    return jnp.where(first, meta[2:3, :], 0.0) + jnp.where(second, meta[3:4, :], 0.0)


def make_meta(routes, gates, place):
    label = lax.broadcasted_iota(jnp.int32, (16, TOK), 0)
    kept = [routes[2 + k : 3 + k, :] == 0 for k in range(2)]
    hit = [jnp.where((routes[k : k + 1, :] == label) & kept[k], 1.0, 0.0).astype(F32) for k in range(2)]
    earlier = lax.broadcasted_iota(jnp.int32, (TOK, TOK), 0) < lax.broadcasted_iota(jnp.int32, (TOK, TOK), 1)
    before = jnp.dot(
        (hit[0] + hit[1]).astype(BF), jnp.where(earlier, 1.0, 0.0).astype(BF), preferred_element_type=F32
    )
    base = place.astype(F32) * CAP
    row = [
        jnp.sum(hit[0] * (before + base), axis=0, keepdims=True),
        jnp.sum(hit[1] * (before + hit[0] + base), axis=0, keepdims=True),
    ]
    out = [jnp.where(kept[k], row[k], -1.0) for k in range(2)]
    out += [jnp.where(kept[k], gates[k : k + 1, :], 0.0) for k in range(2)]
    out.append(jnp.zeros((4, TOK), F32))
    return jnp.concatenate(out, axis=0)


def dispatch_kernel(
    routes, gates, place, tok, cot, rows_tok, rows_cot, metas,
    comp, sendb, meta_send, meta_recv, hop_send, hop_recv, far_send, far_recv, core_send, core_recv,
):
    here = Place()
    metas[0] = make_meta(routes[...], gates[...], place[...])
    barrier(tree_peers(here))
    started = []

    def start(copy):
        copy.start()
        started.append(copy)
        return copy

    for i in range(1, 5):
        depth, way = STEPS[i]
        start(remote(metas.at[0], metas.at[i], meta_send.at[i - 1], meta_recv.at[i - 1], here.near(0, way * depth)))
    source = (tok, cot)
    final = (rows_tok, rows_cot)
    mine = pl.ds(pl.multiple_of(here.core * HALF, HALF), HALF)
    hop = {}

    def first_hop(a):
        for i in (1, 2):
            hop[a, i] = start(
                remote(source[a], comp.at[a, i - 1], hop_send.at[a, i - 1], hop_recv.at[a, i - 1], here.near(0, STEPS[i][1]))
            )

    def second_hop(a, i):
        hop[a, i].wait_recv()
        hop[a, i + 2] = start(
            remote(comp.at[a, i - 1], comp.at[a, i + 1], hop_send.at[a, i + 1], hop_recv.at[a, i + 1], here.near(0, STEPS[i][1]))
        )

    core = {}

    def to_core(a, j):
        part = final[a].at[pl.ds(j * CAP, CAP), mine]
        core[a, j] = start(remote(part, part, core_send.at[a, j], core_recv.at[a, j], here.other_core()))

    far = {}

    def pick(a, i):
        if i >= 3:
            hop[a, i].wait_recv()
        block = source[a] if i == 0 else comp.at[a, i - 1]
        meta = metas[i]
        slots = slots_of(here, i)
        table = plain_table(meta, slots).astype(BF)
        weight = jnp.sum(gate_table(meta, slots), axis=1, keepdims=True) if a else None
        places = [5 + i] + (far_places(i) if i >= 3 else [])

        @pl.loop(0, HALF // COL)
        def _(c):
            cols = pl.ds(pl.multiple_of(c * COL, COL), COL)
            part = jnp.dot(table, block[:, cols], preferred_element_type=F32)
            if a:
                part = part * weight
            part = part.astype(BF)
            home = pl.ds(pl.multiple_of(here.core * HALF + c * COL, COL), COL)
            final[a][pl.ds(i * CAP, CAP), home] = part[:CAP]
            for n, j in enumerate(places):
                sendb[a, j - 5, :, cols] = part[(n + 1) * CAP : (n + 2) * CAP]

        way = STEPS[i][1]
        order = places[1:] + places[:1]
        for j in order:
            if j < 10:
                peer = here.near(1, 0)
            else:
                peer = far_peer(here, way, places.index(j) - 1, 1)
            far[a, j] = start(
                remote(
                    sendb.at[a, j - 5], final[a].at[pl.ds(j * CAP, CAP), mine],
                    far_send.at[a, j - 5], far_recv.at[a, j - 5], peer,
                )
            )
        to_core(a, i)

    metas_done = [False]

    def need_metas():
        if not metas_done[0]:
            for copy in started[:4]:
                copy.wait_recv()
            metas_done[0] = True

    first_hop(0)
    pick(0, 0)
    second_hop(0, 1)
    second_hop(0, 2)
    first_hop(1)
    need_metas()
    pick(0, 1)
    pick(0, 2)
    pick(1, 0)
    pick(0, 3)
    pick(0, 4)
    second_hop(1, 1)
    second_hop(1, 2)
    pick(1, 1)
    pick(1, 2)
    for j in (5, 6, 7, 8, 9, 10, 11, 12, 13, 14, 15):
        far[0, j].wait_recv()
        to_core(0, j)
    pick(1, 3)
    pick(1, 4)
    for j in (5, 6, 7, 8, 9, 10, 11, 12, 13, 14, 15):
        far[1, j].wait_recv()
        to_core(1, j)
    for a in range(2):
        for j in range(16):
            core[a, j].wait_recv()
    for copy in started:
        copy.wait_send()


def dispatch(routes, gates, place, tok, cot):
    vmem = pl.BlockSpec(memory_space=pltpu.VMEM)
    dma = pltpu.SemaphoreType.DMA
    return pl.pallas_call(
        dispatch_kernel,
        out_shape=(
            jax.ShapeDtypeStruct((ROWS, FULL), BF),
            jax.ShapeDtypeStruct((ROWS, FULL), BF),
            jax.ShapeDtypeStruct((5, 8, TOK), F32),
        ),
        in_specs=[vmem] * 5,
        out_specs=(vmem, vmem, vmem),
        scratch_shapes=[
            pltpu.VMEM((2, 4, TOK, HALF), BF),
            pltpu.VMEM((2, 11, CAP, HALF), BF),
            dma((4,)), dma((4,)),
            dma((2, 4)), dma((2, 4)),
            dma((2, 11)), dma((2, 11)),
            dma((2, 16)), dma((2, 16)),
        ],
        compiler_params=pltpu.CompilerParams(
            collective_id=1, has_side_effects=True, vmem_limit_bytes=40 * MIB
        ),
        name="dispatch",
    )(routes, gates, place, tok, cot)


def combine_kernel(
    part_out, part_in, term_gate, term_up, term_down, metas,
    mixed, input_grad, sum_gate, sum_up, sum_down,
    back, beside, distant, two, one, got_two, got_one,
    gu_first, gu_own, gu_mid, gu_home, gu_cross, gu_got,
    dn_first, dn_own, dn_mid, dn_home, dn_cross, dn_got,
    core_send, core_recv, side_send, side_recv, far_send, far_recv, tree_send, tree_recv,
    ring_send, ring_recv, plain_send, plain_recv, mid_send, mid_recv, cross_send, cross_recv, own_sem, home_sem,
):
    here = Place()
    barrier(tree_peers(here) + [here.along_y(1), here.along_y(-1), here.other_xh()])
    started = []

    def start(copy):
        copy.start()
        started.append(copy)
        return copy

    parts = (part_out, part_in)
    theirs = pl.ds(pl.multiple_of((1 - here.core) * HALF, HALF), HALF)
    spans = ((10 * CAP, 6 * CAP), (0, 10 * CAP))
    core = {}
    for a in range(2):
        for n, (at, size) in enumerate(spans):
            core[a, n] = start(
                remote(
                    parts[a].at[pl.ds(at, size), theirs], back.at[a, pl.ds(at, size)],
                    core_send.at[a, n], core_recv.at[a, n], here.other_core(),
                )
            )

    terms = (term_gate, term_up, term_down)
    sums = (sum_gate, sum_up, sum_down)

    def share(p, chunk, half):
        at = pl.ds(pl.multiple_of(chunk * 1024 + half * 512, 512), 512)
        return terms[p].at[:, at] if p == 2 else terms[p].at[at, :]

    def buf(p, gu, dn, *index):
        if p == 2:
            return dn.at[index] if index else dn
        return gu.at[(p,) + index]

    chunk_of = [lax.rem(here.y + 1, 4), lax.rem(here.y + 3, 4)]
    opposite = lax.rem(here.y + 2, 4)
    step = (1, -1)
    ring, plain, mid, cross, own, home = {}, {}, {}, {}, {}, {}
    for p in range(3):
        for w in range(2):
            ring[p, w] = start(
                remote(
                    share(p, opposite, w), buf(p, gu_first, dn_first, w),
                    ring_send.at[p, w], ring_recv.at[p, w], here.along_y(step[w]),
                )
            )
    for p in range(3):
        for w in range(2):
            plain[p, w] = start(
                remote(
                    share(p, chunk_of[w], 1 - w), buf(p, gu_mid, dn_mid, w, 1 - w),
                    plain_send.at[p, w], plain_recv.at[p, w], here.along_y(step[w]),
                )
            )
    for p in range(3):
        for w in range(2):
            own[p, w] = pltpu.make_async_copy(
                share(p, chunk_of[w], w), buf(p, gu_own, dn_own, w), own_sem.at[p, w]
            )
            own[p, w].start()
        for h in range(2):
            home[p, h] = pltpu.make_async_copy(
                share(p, here.y, h), buf(p, gu_home, dn_home, h), home_sem.at[p, h]
            )
            home[p, h].start()

    def by_rows(p, body):
        height = 64

        @pl.loop(0, (FF if p == 2 else 512) // height)
        def _(r):
            body(pl.ds(pl.multiple_of(r * height, height), height))

    def ring_step(p):
        for w in range(2):
            own[p, w].wait()
            ring[p, w].wait_recv()
            a, b = buf(p, gu_own, dn_own, w), buf(p, gu_first, dn_first, w)

            def body(r, a=a, b=b):
                a[r, :] = (a[r, :].astype(F32) + b[r, :].astype(F32)).astype(BF)

            by_rows(p, body)
            mid[p, w] = start(
                remote(
                    a, buf(p, gu_mid, dn_mid, w, w), mid_send.at[p, w], mid_recv.at[p, w],
                    here.along_y(step[w]),
                )
            )

    def cross_step(p):
        for w in range(2):
            home[p, w].wait()
            plain[p, w].wait_recv()
            mid[p, w].wait_recv()
        away = 1 - here.xh
        a, b, c = buf(p, gu_home, dn_home, away), buf(p, gu_mid, dn_mid, 0, away), buf(p, gu_mid, dn_mid, 1, away)
        d = buf(p, gu_cross, dn_cross)

        def body(r):
            d[r, :] = (a[r, :].astype(F32) + b[r, :].astype(F32) + c[r, :].astype(F32)).astype(BF)

        by_rows(p, body)
        cross[p] = start(
            remote(d, buf(p, gu_got, dn_got), cross_send.at[p], cross_recv.at[p], here.other_xh())
        )

    def last_step(p):
        cross[p].wait_recv()
        a = buf(p, gu_home, dn_home, here.xh)
        b, c = buf(p, gu_mid, dn_mid, 0, here.xh), buf(p, gu_mid, dn_mid, 1, here.xh)
        d = buf(p, gu_got, dn_got)
        out = sums[p]

        def body(r):
            total = a[r, :].astype(F32) + b[r, :].astype(F32) + c[r, :].astype(F32) + d[r, :].astype(F32)
            out[r, :] = total.astype(BF)

        by_rows(p, body)

    def add_halves(a, n):
        core[a, n].wait_recv()
        at, size = spans[n]

        @pl.loop(0, size // CAP)
        def _(r):
            rows = pl.ds(pl.multiple_of(at + r * CAP, CAP), CAP)

            @pl.loop(0, HALF // COL)
            def _(c):
                cols = pl.ds(pl.multiple_of(c * COL, COL), COL)
                own_cols = pl.ds(pl.multiple_of(here.core * HALF + c * COL, COL), COL)
                total = parts[a][rows, own_cols].astype(F32) + back[a, rows, cols].astype(F32)
                back[a, rows, cols] = total.astype(BF)

    side, far, tree = {}, {}, {}

    def send_rows(a):
        add_halves(a, 0)
        for way in (1, -1):
            for n in range(3):
                w = 0 if way == 1 else 1
                j = FAR[(way, n)]
                far[a, w, n] = start(
                    remote(
                        back.at[a, pl.ds(j * CAP, CAP)], distant.at[a, w, n],
                        far_send.at[a, w, n], far_recv.at[a, w, n], far_peer(here, way, n, -1),
                    )
                )
        add_halves(a, 1)
        for i in (3, 4, 1, 2, 0):
            side[a, i] = start(
                remote(
                    back.at[a, pl.ds((5 + i) * CAP, CAP)], beside.at[a, i],
                    side_send.at[a, i], side_recv.at[a, i], here.near(1, 0),
                )
            )

    def spread(a, i, more, out):
        side[a, i].wait_recv()
        meta = metas[i]
        slots = slots_of(here, i)
        if a:
            tables = [plain_table(meta, slots).astype(BF)]
        else:
            exact = gate_table(meta, slots)
            high = exact.astype(BF)
            tables = [high, (exact - high.astype(F32)).astype(BF)]

        @pl.loop(0, HALF // COL)
        def _(c):
            cols = pl.ds(pl.multiple_of(c * COL, COL), COL)
            rows = [back[a, pl.ds(i * CAP, CAP), cols], beside[a, i, :, cols]]
            if i >= 3:
                rows += [distant[a, i - 3, n, :, cols] for n in range(3)]
            rows = jnp.concatenate(rows, axis=0)
            total = None
            for table in tables:
                term = lax.dot_general(table, rows, (((0,), (0,)), ((), ())), preferred_element_type=F32)
                total = term if total is None else total + term
            for ref in more:
                total = total + ref[:, cols].astype(F32)
            out[:, cols] = total.astype(BF)

    def sum_two(a):
        for w in range(2):
            for n in range(3):
                far[a, w, n].wait_recv()
            spread(a, 3 + w, [], two.at[a, w])
            tree[a, w] = start(
                remote(
                    two.at[a, w], got_two.at[a, w], tree_send.at[a, w], tree_recv.at[a, w], here.near(0, -step[w])
                )
            )

    def sum_one(a):
        for w in range(2):
            tree[a, w].wait_recv()
            spread(a, 1 + w, [got_two.at[a, w]], one.at[a, w])
            tree[a, 2 + w] = start(
                remote(
                    one.at[a, w], got_one.at[a, w], tree_send.at[a, 2 + w], tree_recv.at[a, 2 + w],
                    here.near(0, -step[w]),
                )
            )

    def sum_home(a, out):
        for w in range(2):
            tree[a, 2 + w].wait_recv()
        spread(a, 0, [got_one.at[a, 0], got_one.at[a, 1]], out)

    send_rows(0)
    send_rows(1)
    ring_step(0)
    sum_two(0)
    ring_step(1)
    sum_two(1)
    ring_step(2)
    sum_one(0)
    sum_one(1)
    cross_step(0)
    sum_home(0, mixed)
    cross_step(1)
    sum_home(1, input_grad)
    last_step(0)
    cross_step(2)
    last_step(1)
    last_step(2)
    for copy in started:
        copy.wait_send()


def combine(part_out, part_in, term_gate, term_up, term_down, metas):
    vmem = pl.BlockSpec(memory_space=pltpu.VMEM)
    hbm = pl.BlockSpec(memory_space=pl.ANY)
    dma = pltpu.SemaphoreType.DMA
    return pl.pallas_call(
        combine_kernel,
        out_shape=(
            jax.ShapeDtypeStruct((TOK, HALF), BF),
            jax.ShapeDtypeStruct((TOK, HALF), BF),
            jax.ShapeDtypeStruct((512, FF), BF),
            jax.ShapeDtypeStruct((512, FF), BF),
            jax.ShapeDtypeStruct((FF, 512), BF),
        ),
        in_specs=[vmem, vmem, hbm, hbm, hbm, vmem],
        out_specs=(vmem,) * 5,
        scratch_shapes=[
            pltpu.VMEM((2, ROWS, HALF), BF),
            pltpu.VMEM((2, 5, CAP, HALF), BF),
            pltpu.VMEM((2, 2, 3, CAP, HALF), BF),
            pltpu.VMEM((2, 2, TOK, HALF), BF),
            pltpu.VMEM((2, 2, TOK, HALF), BF),
            pltpu.VMEM((2, 2, TOK, HALF), BF),
            pltpu.VMEM((2, 2, TOK, HALF), BF),
            pltpu.VMEM((2, 2, 512, FF), BF),
            pltpu.VMEM((2, 2, 512, FF), BF),
            pltpu.VMEM((2, 2, 2, 512, FF), BF),
            pltpu.VMEM((2, 2, 512, FF), BF),
            pltpu.VMEM((2, 512, FF), BF),
            pltpu.VMEM((2, 512, FF), BF),
            pltpu.VMEM((2, FF, 512), BF),
            pltpu.VMEM((2, FF, 512), BF),
            pltpu.VMEM((2, 2, FF, 512), BF),
            pltpu.VMEM((2, FF, 512), BF),
            pltpu.VMEM((FF, 512), BF),
            pltpu.VMEM((FF, 512), BF),
            dma((2, 2)), dma((2, 2)),
            dma((2, 5)), dma((2, 5)),
            dma((2, 2, 3)), dma((2, 2, 3)),
            dma((2, 4)), dma((2, 4)),
            dma((3, 2)), dma((3, 2)),
            dma((3, 2)), dma((3, 2)),
            dma((3, 2)), dma((3, 2)),
            dma((3,)), dma((3,)),
            dma((3, 2)), dma((3, 2)),
        ],
        compiler_params=pltpu.CompilerParams(
            collective_id=2, has_side_effects=True, vmem_limit_bytes=56 * MIB
        ),
        name="combine",
    )(part_out, part_in, term_gate, term_up, term_down, metas)


def per_device(tokens, routes, gates, dropped, placement, w_gate, w_up, w_down, cotangent):
    table = jnp.concatenate([routes.T, dropped.T], axis=0)
    place = jnp.broadcast_to(jnp.pad(placement, (0, 1))[:, None], (16, TOK))
    rows, grads, metas = dispatch(table, gates.T, place, tokens, cotangent)
    gate_matrix, up_matrix, down_matrix = w_gate[0], w_up[0], w_down[0]
    gate_pre = jnp.dot(rows, gate_matrix, preferred_element_type=F32)
    up_pre = jnp.dot(rows, up_matrix, preferred_element_type=F32)
    sigmoid_gate = jax.nn.sigmoid(gate_pre)
    silu_gate = gate_pre * sigmoid_gate
    hidden = (silu_gate * up_pre).astype(BF)
    part_out = jnp.dot(hidden, down_matrix, preferred_element_type=F32).astype(BF)
    contract = (((1,), (1,)), ((), ()))
    grad_hidden = lax.dot_general(grads, down_matrix, contract, preferred_element_type=F32)
    slope = sigmoid_gate * (1.0 + gate_pre * (1.0 - sigmoid_gate))
    grad_gate_pre = (grad_hidden * up_pre * slope).astype(BF)
    grad_up_pre = (grad_hidden * silu_gate).astype(BF)
    part_in = lax.dot_general(grad_gate_pre, gate_matrix, contract, preferred_element_type=F32)
    part_in = part_in + lax.dot_general(grad_up_pre, up_matrix, contract, preferred_element_type=F32)
    along_rows = (((0,), (0,)), ((), ()))
    term_gate = lax.dot_general(rows, grad_gate_pre, along_rows, preferred_element_type=F32).astype(BF)
    term_up = lax.dot_general(rows, grad_up_pre, along_rows, preferred_element_type=F32).astype(BF)
    term_down = lax.dot_general(hidden, grads, along_rows, preferred_element_type=F32).astype(BF)
    mixed, input_grad, grad_gate, grad_up, grad_down = combine(
        part_out, part_in.astype(BF), term_gate, term_up, term_down, metas
    )
    return mixed, input_grad, grad_gate[None], grad_up[None], grad_down[None]


def solution(mesh):
    in_specs = (
        P(("dp", "expert"), "tensor"),
        P(("dp", "expert"), None),
        P(("dp", "expert"), None),
        P(("dp", "expert"), None),
        P(),
        P("expert", None, "tensor"),
        P("expert", None, "tensor"),
        P("expert", "tensor", None),
        P(("dp", "expert"), "tensor"),
    )
    out_specs = (
        P(("dp", "expert"), "tensor"),
        P(("dp", "expert"), "tensor"),
        P("expert", "dp", "tensor"),
        P("expert", "dp", "tensor"),
        P("expert", "tensor", "dp"),
    )
    return jax.shard_map(
        per_device, mesh=mesh, in_specs=in_specs, out_specs=out_specs, check_vma=False
    )
```

time: 375 us -> 232 us (0.62)
  Pallas kernels: 0 us -> 185 us
  waiting for transfers between devices: 153 us -> 0 us
  blocking collectives: 110 us -> 0 us
  other arithmetic: 19.3 us -> 0.77 us
  starting transfers between devices: 14.4 us -> 0 us
  between operations: 14 us -> 0.74 us
  local copies, waits for them, and re-layouts: 23.5 us -> 12.8 us
  matrix products: 39.6 us -> 32.1 us
    pallas_call x0 -> x2, Pallas kernels: none -> 185 us  [the longest x1 99.1 us: combine(): pl.pallas_call(combine_kernel, out_shape=(jax.ShapeDtypeStruct((TOK, HALF...]
    all_to_all x2 -> x0, blocking collectives: 110 us -> none  [the longest x1 57.4 us: per_device(): lax.all_to_all(token_send, 'expert', split_axis=0, concat_axis=0, tiled=T...]
    all_to_all x2 -> x0, waiting for transfers between devices: 85.1 us -> none  [the longest x1 46.8 us: per_device(): lax.all_to_all(input_half, 'expert', split_axis=0, concat_axis=0, tiled=T...]
    reduce_scatter x3 -> x0, waiting for transfers between devices: 56.9 us -> none  [the longest x1 46.7 us: per_device(): lax.psum_scatter(jnp.concatenate([gate_term, up_term, down_term], axis=1)...]
    all_to_all x2 -> x0, starting transfers between devices: 14 us -> none  [the longest x1 7.44 us: per_device(): lax.all_to_all(out_half, 'expert', split_axis=0, concat_axis=0, tiled=True)]
    all_gather x2 -> x0, waiting for transfers between devices: 11.2 us -> none  [the longest x1 11.2 us: per_device(): grad_in = lax.all_gather(got_grads, 'tensor', axis=2, tiled=True)]
    reduce_sum x4 -> x0, other arithmetic: 11.1 us -> none  [the longest x2 10.2 us: gather_routes(): return jnp.sum(scaled.reshape(-1, route_count, features), axis=1)]
    gather x2 -> x0, local copies, waits for them, and re-layouts: 6.55 us -> none  [gather_routes(): jnp.take(flat_back, jnp.maximum(buffer_row, 0), axis=0).astype(jnp.float32)]
  transfers between devices with their start and end apart: 7 -> 0, of which waited for: 5 -> 0; matrix products, arithmetic and copies ran while one was open for 15% -> 0% of each run, Pallas kernels for 0% -> 0%
where the time goes in v1:
time: 232 us; the launch traced here: 231 us
  Pallas kernels  185 us (80%)
  matrix products  32.1 us (14%)
  local copies, waits for them, and re-layouts  12.8 us (6%)
    pallas_call x1, Pallas kernels, combine(): pl.pallas_call(combine_kernel, out_shape=(jax.ShapeDtypeStruct((TOK, HALF...  99.1 us
    pallas_call x1, Pallas kernels, dispatch(): pl.pallas_call(dispatch_kernel, out_shape=(jax.ShapeDtypeStruct((ROWS, FU...  85.6 us
    unnamed x19, local copies, waits for them, and re-layouts  11.9 us

profile of v1, /device:TPU:1, one launch (start us, length us, event | category | flops | bytes accessed | tf_op | source)
XLA Modules:
  0.0 231.1 jit_solution(6163007851093990340)
XLA Ops:
  0.6 0.0 copy-start
  0.6 0.8 pad.4
  1.5 0.1 broadcast_in_dim.15.place
  1.5 0.8 pad_add_fusion.routes
  2.3 0.0 copy-start.1
  2.3 1.0 copy-done.1
  3.3 0.0 copy-start.2
  3.3 1.0 copy-done.2
  4.4 0.7 copy-done.4
  5.1 85.6 %dispatch.1 = (bf16[512,4096]{1,0:T(8,128)(2,1)S(1)}, bf16[512,4096]{1,0:T(8,128)(2,1)S(1)}, f32[5,8,128]{2,1,0:T(8,128)S(1)}) custom-call(s32[4,128]{1,0:T(4,128)S(1)} %pad_add_fusion.routes, f32[2,128]{1,0:T(2,128)S(1)} %bitcast.35, s32[16,128]{1,0:T(8,128)S(1)} %broadcast_in_dim.15.place, bf16[128,2048]{1,0:T(8,128)(2,1)S(1)} %copy-done.1, ...), custom_call_target="tpu_custom_call" | custom-call | tf_op jit(solution)/shard_map/dispatch/pallas_call | solution.py:248
  90.6 0.0 copy-start.3
  90.6 0.0 copy-start.5
  90.7 4.4 %fusion.4 = f32[512,384]{1,0:T(8,128)S(1)} fusion(bf16[512,4096]{1,0:T(8,128)(2,1)S(1)} %get-tuple-element.13, bf16[1,4096,384]{2,1,0:T(8,128)(2,1)} %param.15), kind=kOutput, calls=%fused_computation.9 | convolution fusion | flops 1610612736 | bytes 8126464 | tf_op jit(solution)/shard_map/dot_general | solution.py:571
  95.0 0.0 copy-done.3
  95.0 0.0 copy-done.5
  95.0 2.3 %fusion.8 = f32[512,384]{1,0:T(8,128)S(1)} fusion(bf16[512,4096]{1,0:T(8,128)(2,1)S(1)} %get-tuple-element.13, bf16[1,4096,384]{2,1,0:T(8,128)(2,1)S(1)} %copy-done.5), kind=kOutput, calls=%fused_computation.13 | convolution fusion | flops 1610612736 | bytes 8126464 | tf_op jit(solution)/shard_map/dot_general | solution.py:570
  97.4 0.0 copy-done
  97.4 2.5 %multiply_convert_fusion = (bf16[512,384]{1,0:T(8,128)(2,1)S(1)}, bf16[512,384]{1,0:T(8,128)(2,1)S(1)}, bf16[512,384]{1,0:T(8,128)(2,1)S(1)}) fusion(f32[512,384]{1,0:T(8,128)S(1)} %fusion.8, f32[512,384]{1,0:T(8,128)S(1)} %fusion.4, bf16[512,4096]{1,0:T(8,128)(2,1)S(1)} %get-tuple-element.14, bf16[1,384,4096]{2,1,0:T(8,128)(2,1)S(1)} %copy-done), kind=kOutput, calls=%fused_computation.15 | convolution fusion | flops 1613561856 | bytes 10092544 | tf_op jit(solution)/shard_map/dot_general | solution.py:577
  99.9 0.0 copy-start.6
  99.9 2.4 %fusion.6 = f32[512,4096]{1,0:T(8,128)S(1)} fusion(bf16[512,384]{1,0:T(8,128)(2,1)S(1)} %get-tuple-element.22, bf16[1,4096,384]{2,1,0:T(8,128)(2,1)S(1)} %copy-done.5), kind=kOutput, calls=%fused_computation.11 | convolution fusion | flops 1610612736 | bytes 11927552 | tf_op jit(solution)/shard_map/dot_general | solution.py:581
  102.3 0.0 copy-done.6
  102.3 4.4 %add_convert_fusion.part_in = bf16[512,4096]{1,0:T(8,128)(2,1)} fusion(f32[512,4096]{1,0:T(8,128)S(1)} %fusion.6, bf16[512,384]{1,0:T(8,128)(2,1)S(1)} %get-tuple-element.21, bf16[1,4096,384]{2,1,0:T(8,128)(2,1)S(1)} %copy-done.6), kind=kOutput, calls=%fused_computation | convolution fusion | flops 1614807040 | bytes 16121856 | tf_op jit(solution)/shard_map/dot_general | solution.py:582
  106.7 4.1 %convolution_convert_fusion.2.term_up = bf16[4096,384]{1,0:T(8,128)(2,1)} fusion(bf16[512,4096]{1,0:T(8,128)(2,1)S(1)} %get-tuple-element.13, bf16[512,384]{1,0:T(8,128)(2,1)S(1)} %get-tuple-element.21), kind=kOutput, calls=%fused_computation.3 | convolution fusion | flops 1612185600 | bytes 7733248 | tf_op jit(solution)/shard_map/dot_general | solution.py:585
  110.8 4.3 %convolution_convert_fusion.3.term_gate = bf16[4096,384]{1,0:T(8,128)(2,1)} fusion(bf16[512,4096]{1,0:T(8,128)(2,1)S(1)} %get-tuple-element.13, bf16[512,384]{1,0:T(8,128)(2,1)S(1)} %get-tuple-element.22), kind=kOutput, calls=%fused_computation.4 | convolution fusion | flops 1612185600 | bytes 7733248 | tf_op jit(solution)/shard_map/dot_general | solution.py:584
  115.1 3.5 %convolution_convert_fusion.1.term_down = bf16[384,4096]{1,0:T(8,128)(2,1)} fusion(bf16[512,384]{1,0:T(8,128)(2,1)S(1)} %get-tuple-element.23, bf16[512,4096]{1,0:T(8,128)(2,1)S(1)} %get-tuple-element.14), kind=kOutput, calls=%fused_computation.2 | convolution fusion | flops 1612185600 | bytes 7733248 | tf_op jit(solution)/shard_map/dot_general | solution.py:586
  118.6 4.3 %convolution_convert_fusion.part_out = bf16[512,4096]{1,0:T(8,128)(2,1)} fusion(bf16[512,384]{1,0:T(8,128)(2,1)S(1)} %get-tuple-element.23, bf16[1,384,4096]{2,1,0:T(8,128)(2,1)S(1)} %copy-done), kind=kOutput, calls=%fused_computation.1 | convolution fusion | flops 1612709888 | bytes 7733248 | tf_op jit(solution)/shard_map/dot_general | solution.py:575
  122.8 99.1 %combine.1 = (bf16[128,2048]{1,0:T(8,128)(2,1)}, bf16[128,2048]{1,0:T(8,128)(2,1)}, bf16[512,384]{1,0:T(8,128)(2,1)}, bf16[512,384]{1,0:T(8,128)(2,1)}, bf16[384,512]{1,0:T(8,128)(2,1)}) custom-call(bf16[512,4096]{1,0:T(8,128)(2,1)} %convolution_convert_fusion.part_out, bf16[512,4096]{1,0:T(8,128)(2,1)} %add_convert_fusion.part_in, ...), custom_call_target="tpu_custom_call" | custom-call | tf_op jit(solution)/shard_map/combine/pallas_call | solution.py:517
  222.0 1.9 copy.19
  223.9 1.9 copy.20
  225.8 1.8 copy.21
  227.5 1.8 copy.22
  229.3 1.8 copy.23
  (1 shorter events, 0.0 us)
Async XLA Ops:
  0.6 96.7 %copy-start = (bf16[1,384,4096]{2,1,0:T(8,128)(2,1)S(1)}, bf16[1,384,4096]{2,1,0:T(8,128)(2,1)}, u32[]{:S(2)}) copy-start(bf16[1,384,4096]{2,1,0:T(8,128)(2,1)} %param.16) | copy-start | bytes 9437188
  2.3 1.0 copy-start.1
  3.3 1.0 copy-start.2
  4.4 0.7 copy-start.4
  90.6 4.4 %copy-start.3 = (f32[5,8,128]{2,1,0:T(8,128)}, f32[5,8,128]{2,1,0:T(8,128)S(1)}, u32[]{:S(2)}) copy-start(f32[5,8,128]{2,1,0:T(8,128)S(1)} %get-tuple-element.15.metas) | copy-start | bytes 61444
  90.6 4.4 %copy-start.5 = (bf16[1,4096,384]{2,1,0:T(8,128)(2,1)S(1)}, bf16[1,4096,384]{2,1,0:T(8,128)(2,1)}, u32[]{:S(2)}) copy-start(bf16[1,4096,384]{2,1,0:T(8,128)(2,1)} %param.14) | copy-start | bytes 9437188
  99.9 2.4 %copy-start.6 = (bf16[1,4096,384]{2,1,0:T(8,128)(2,1)S(1)}, bf16[1,4096,384]{2,1,0:T(8,128)(2,1)}, u32[]{:S(2)}) copy-start(bf16[1,4096,384]{2,1,0:T(8,128)(2,1)} %param.15) | copy-start | bytes 9437188

commit v2 on v1

v2 whole, which is shorter than its diff:
```python
import jax
import jax.numpy as jnp
from jax import lax
from jax.experimental import pallas as pl
from jax.experimental.pallas import tpu as pltpu
from jax.sharding import PartitionSpec as P

MESH = pl.DeviceIdType.MESH
BF = jnp.bfloat16
F32 = jnp.float32
TOK = 128
CAP = 32
ROWS = 16 * CAP
FULL = 4096
HALF = 2048
FF = 384
COL = 512
MIB = 1 << 20

STEPS = ((0, 0), (1, 1), (1, -1), (2, 1), (2, -1))
FAR = {(1, 0): 10, (1, 1): 11, (-1, 0): 12, (-1, 1): 13, (1, 2): 14, (-1, 2): 15}


class Place:
    def __init__(self):
        self.dp = lax.axis_index("dp")
        expert = lax.axis_index("expert")
        self.core = lax.axis_index("tensor")
        self.y = lax.div(self.dp, 2)
        self.xh = lax.rem(self.dp, 2)
        self.x = lax.div(expert, 8)
        self.z = lax.rem(expert, 8)

    def slot(self, dx, dz):
        return lax.rem(self.x + dx, 2) * 8 + lax.rem(self.z + dz + 8, 8)

    def near(self, dx, dz):
        return (self.dp, self.slot(dx, dz), self.core)

    def other_core(self):
        return (self.dp, self.slot(0, 0), 1 - self.core)

    def along_y(self, dy):
        return (lax.rem(self.y + dy + 4, 4) * 2 + self.xh, self.slot(0, 0), self.core)

    def other_xh(self):
        return (self.y * 2 + 1 - self.xh, self.slot(0, 0), self.core)


def barrier(peers):
    sem = pltpu.get_barrier_semaphore()
    for peer in peers:
        pl.semaphore_signal(sem, inc=1, device_id=peer, device_id_type=MESH)
    pl.semaphore_wait(sem, len(peers))


def tree_peers(here):
    return [
        here.near(0, 1), here.near(0, -1), here.near(0, 2), here.near(0, -2), here.near(1, 0),
        here.near(1, 1), here.near(1, -1), here.near(1, 2), here.near(1, -2), here.other_core(),
    ]


def remote(src, dst, send, recv, peer):
    return pltpu.make_async_remote_copy(
        src_ref=src, dst_ref=dst, send_sem=send, recv_sem=recv, device_id=peer, device_id_type=MESH
    )


def slots_of(here, index):
    slots = [here.slot(0, 0), here.slot(1, 0)]
    depth, way = STEPS[index]
    if depth == 2:
        slots += [here.slot(0, way), here.slot(1, way)]
        slots.append(here.slot(0, 2) if way == 1 else here.slot(1, -2))
    return slots


def far_places(index):
    way = STEPS[index][1]
    return [FAR[(way, n)] for n in range(3)]


def far_peer(here, way, n, sign):
    if n == 0:
        return here.near(0, way * sign)
    if n == 1:
        return here.near(1, way * sign)
    return here.near(0, 2 * sign) if way == 1 else here.near(1, -2 * sign)


def hits(meta, slots):
    ids = jnp.concatenate(
        [(s * CAP + lax.broadcasted_iota(jnp.int32, (CAP, TOK), 0)).astype(F32) for s in slots], axis=0
    )
    return meta[0:1, :] == ids, meta[1:2, :] == ids


def plain_table(meta, slots):
    first, second = hits(meta, slots)
    return jnp.where(first | second, 1.0, 0.0).astype(F32)


def gate_table(meta, slots):
    first, second = hits(meta, slots)
    return jnp.where(first, meta[2:3, :], 0.0) + jnp.where(second, meta[3:4, :], 0.0)


def make_meta(routes, gates, dropped, placement):
    row = lax.broadcasted_iota(jnp.int32, (TOK, TOK), 0)
    column = lax.broadcasted_iota(jnp.int32, (TOK, TOK), 1)
    route = [routes[k : k + 1, :] for k in range(2)]
    kept = [dropped[k : k + 1, :] == 0 for k in range(2)]
    gate = [gates[k : k + 1, :] for k in range(2)]
    label = lax.broadcasted_iota(jnp.int32, (16, TOK), 0)
    base = jnp.zeros((16, TOK), F32)
    for e in range(15):
        base = jnp.where(label == e, (placement[e] * CAP).astype(F32), base)
    hit = [jnp.where((route[k] == label) & kept[k], 1.0, 0.0).astype(F32) for k in range(2)]
    before = jnp.dot(
        (hit[0] + hit[1]).astype(BF), jnp.where(row < column, 1.0, 0.0).astype(BF), preferred_element_type=F32
    )
    at = [
        jnp.sum(hit[0] * (before + base), axis=0, keepdims=True),
        jnp.sum(hit[1] * (before + hit[0] + base), axis=0, keepdims=True),
    ]
    out = [jnp.where(kept[k], at[k], -1.0) for k in range(2)]
    out += [jnp.where(kept[k], gate[k], 0.0) for k in range(2)]
    out.append(jnp.zeros((4, TOK), F32))
    return jnp.concatenate(out, axis=0)


NT = (((1,), (1,)), ((), ()))


def layer_kernel(
    tok, cot, routes, gates, dropped, placement, w_gate, w_up, w_down,
    mixed, input_grad, sum_gate, sum_up, sum_down,
    tokv, cotv, metas, comp, sendb, rows_tok, rows_cot, wide, down, pre, hidden, slopes, terms,
    back, beside, distant, got_two, got_one, first, middle, got,
    meta_send, meta_recv, hop_send, hop_recv, row_send, row_recv, pair_send, pair_recv,
    core_send, core_recv, side_send, side_recv, far_send, far_recv, tree_send, tree_recv,
    ring_send, ring_recv, plain_send, plain_recv, mid_send, mid_recv, cross_send, cross_recv, load_sem,
):
    here = Place()
    waiting = []

    def start(copy):
        copy.start()
        waiting.append(copy)
        return copy

    def sent(copy):
        waiting[:] = [other for other in waiting if other is not copy]
        copy.wait_send()

    loads = [
        pltpu.make_async_copy(tok, tokv, load_sem.at[0]),
        pltpu.make_async_copy(cot, cotv, load_sem.at[1]),
        pltpu.make_async_copy(w_gate, wide.at[:, pl.ds(0, FF)], load_sem.at[2]),
        pltpu.make_async_copy(w_up, wide.at[:, pl.ds(FF, FF)], load_sem.at[3]),
        pltpu.make_async_copy(w_down, down, load_sem.at[4]),
    ]
    barrier(tree_peers(here) + [here.along_y(1), here.along_y(-1), here.other_xh()])
    loads[0].start()

    source = (tok, cot)
    local = (tokv, cotv)
    final = (rows_tok, rows_cot)
    mine = pl.ds(pl.multiple_of(here.core * HALF, HALF), HALF)
    theirs = pl.ds(pl.multiple_of((1 - here.core) * HALF, HALF), HALF)
    hop, row, pair = {}, {}, {}

    def first_hop(a):
        for i in (1, 2):
            hop[a, i] = start(
                remote(source[a], comp.at[a, i - 1], hop_send.at[a, i - 1], hop_recv.at[a, i - 1], here.near(0, STEPS[i][1]))
            )

    def second_hop(a):
        for i in (1, 2):
            hop[a, i].wait_recv()
            hop[a, i + 2] = start(
                remote(comp.at[a, i - 1], comp.at[a, i + 1], hop_send.at[a, i + 1], hop_recv.at[a, i + 1], here.near(0, STEPS[i][1]))
            )

    def to_core(a, j):
        part = final[a].at[pl.ds(j * CAP, CAP), mine]
        pair[a, j] = start(remote(part, part, pair_send.at[a, j], pair_recv.at[a, j], here.other_core()))

    def pick(a, i):
        if i >= 3:
            hop[a, i].wait_recv()
        block = local[a] if i == 0 else comp.at[a, i - 1]
        meta = metas[i]
        slots = slots_of(here, i)
        table = plain_table(meta, slots).astype(BF)
        weight = jnp.sum(gate_table(meta, slots), axis=1, keepdims=True) if a else None
        places = [5 + i] + (far_places(i) if i >= 3 else [])

        @pl.loop(0, HALF // COL)
        def _(c):
            cols = pl.ds(pl.multiple_of(c * COL, COL), COL)
            part = jnp.dot(table, block[:, cols], preferred_element_type=F32)
            if a:
                part = part * weight
            part = part.astype(BF)
            home = pl.ds(pl.multiple_of(here.core * HALF + c * COL, COL), COL)
            final[a][pl.ds(i * CAP, CAP), home] = part[:CAP]
            for n, j in enumerate(places):
                sendb[a, j - 5, :, cols] = part[(n + 1) * CAP : (n + 2) * CAP]

        way = STEPS[i][1]
        for j in places[1:] + places[:1]:
            peer = here.near(1, 0) if j < 10 else far_peer(here, way, places.index(j) - 1, 1)
            row[a, j] = start(
                remote(
                    sendb.at[a, j - 5], final[a].at[pl.ds(j * CAP, CAP), mine],
                    row_send.at[a, j - 5], row_recv.at[a, j - 5], peer,
                )
            )
        to_core(a, i)

    def collect(a):
        for j in (5, 6, 7, 8, 9, 10, 11, 12, 13, 14, 15):
            row[a, j].wait_recv()
            to_core(a, j)

    def whole(a):
        for j in range(16):
            pair[a, j].wait_recv()

    def forward(r):
        rows = pl.ds(r * 256, 256)

        @pl.loop(0, 3)
        def _(c):
            cols = pl.ds(pl.multiple_of(c * 256, 256), 256)
            pre[rows, cols] = jnp.dot(rows_tok[rows, :], wide[:, cols], preferred_element_type=F32)

    def activate():
        @pl.loop(0, ROWS // 64)
        def _(r):
            rows = pl.ds(pl.multiple_of(r * 64, 64), 64)
            gate = pre[rows, :FF]
            hidden[rows, :] = (gate * jax.nn.sigmoid(gate) * pre[rows, FF:]).astype(BF)

    def forward_out():
        @pl.loop(0, FULL // 256)
        def _(c):
            cols = pl.ds(pl.multiple_of(c * 256, 256), 256)
            terms[pl.ds(0, ROWS), cols] = jnp.dot(
                hidden[...], down[:, cols], preferred_element_type=F32
            ).astype(BF)

    def backward_hidden():
        @pl.loop(0, 4)
        def _(r):
            rows = pl.ds(pl.multiple_of(r * 128, 128), 128)
            grad = lax.dot_general(rows_cot[rows, :], down[...], NT, preferred_element_type=F32)
            gate, up = pre[rows, :FF], pre[rows, FF:]
            sigmoid = jax.nn.sigmoid(gate)
            slope = sigmoid * (1.0 + gate * (1.0 - sigmoid))
            slopes[rows, :FF] = (grad * up * slope).astype(BF)
            slopes[rows, FF:] = (grad * (gate * sigmoid)).astype(BF)

    def backward_rows():
        both = slopes[...]

        @pl.loop(0, FULL // 256)
        def _(c):
            cols = pl.ds(pl.multiple_of(c * 256, 256), 256)
            rows_tok[:, cols] = lax.dot_general(both, wide[cols, :], NT, preferred_element_type=F32).astype(BF)

    chunk_of = [lax.rem(here.y + 1, 4), lax.rem(here.y + 3, 4)]
    opposite = lax.rem(here.y + 2, 4)
    step = (1, -1)
    sums = (sum_gate, sum_up, sum_down)
    ring, plain, mid, cross = {}, {}, {}, {}

    def share(p, chunk, half):
        return terms.at[pl.ds(p * FF, FF), pl.ds(pl.multiple_of(chunk * 1024 + half * 512, 512), 512)]

    def weight_terms(pieces, small, big):
        at, size = pieces[0] * FF, len(pieces) * FF
        turned = small[...].T

        def chunk_terms(chunk):
            @pl.loop(0, 4)
            def _(c):
                cols = pl.ds(pl.multiple_of(chunk * 1024 + c * 256, 256), 256)
                terms[pl.ds(at, size), cols] = jnp.dot(turned, big[:, cols], preferred_element_type=F32).astype(BF)

        chunk_terms(opposite)
        for p in pieces:
            for w in range(2):
                ring[p, w] = start(
                    remote(
                        share(p, opposite, w), first.at[p, w],
                        ring_send.at[p, w], ring_recv.at[p, w], here.along_y(step[w]),
                    )
                )
        chunk_terms(chunk_of[0])
        chunk_terms(chunk_of[1])
        for p in pieces:
            for w in range(2):
                plain[p, w] = start(
                    remote(
                        share(p, chunk_of[w], 1 - w), middle.at[p, w, 1 - w],
                        plain_send.at[p, w], plain_recv.at[p, w], here.along_y(step[w]),
                    )
                )
        chunk_terms(here.y)

    def by_rows(body, height=64):
        @pl.loop(0, FF // height)
        def _(r):
            body(pl.ds(pl.multiple_of(r * height, height), height))

    def ring_step(p):
        for w in range(2):
            ring[p, w].wait_recv()
            a, b = share(p, chunk_of[w], w), first.at[p, w]

            def body(r, a=a, b=b):
                a[r, :] = (a[r, :].astype(F32) + b[r, :].astype(F32)).astype(BF)

            by_rows(body)
            mid[p, w] = start(
                remote(a, middle.at[p, w, w], mid_send.at[p, w], mid_recv.at[p, w], here.along_y(step[w]))
            )

    def cross_step(p):
        for w in range(2):
            plain[p, w].wait_recv()
            mid[p, w].wait_recv()
        away = 1 - here.xh
        a, b, c = share(p, here.y, away), middle.at[p, 0, away], middle.at[p, 1, away]

        def body(r):
            a[r, :] = (a[r, :].astype(F32) + b[r, :].astype(F32) + c[r, :].astype(F32)).astype(BF)

        by_rows(body)
        cross[p] = start(remote(a, got.at[p], cross_send.at[p], cross_recv.at[p], here.other_xh()))

    def last_step(p):
        cross[p].wait_recv()
        a, b, c = share(p, here.y, here.xh), middle.at[p, 0, here.xh], middle.at[p, 1, here.xh]
        for n in range(3):
            r = pl.ds(n * 128, 128)
            total = a[r, :].astype(F32) + b[r, :].astype(F32) + c[r, :].astype(F32) + got[p, r, :].astype(F32)
            if p == 2:
                sums[p][r, :] = total.astype(BF)
            else:
                sums[p][:, r] = total.T.astype(BF)

    parts = (terms, rows_tok)
    spans = ((10 * CAP, 6 * CAP), (0, 10 * CAP))
    core, side, far, tree = {}, {}, {}, {}

    def swap_halves(a):
        for n, (at, size) in enumerate(spans):
            core[a, n] = start(
                remote(
                    parts[a].at[pl.ds(at, size), theirs], back.at[a, pl.ds(at, size)],
                    core_send.at[a, n], core_recv.at[a, n], here.other_core(),
                )
            )

    def add_halves(a, n):
        core[a, n].wait_recv()
        at, size = spans[n]

        @pl.loop(0, size // CAP)
        def _(r):
            rows = pl.ds(pl.multiple_of(at + r * CAP, CAP), CAP)
            total = parts[a][rows, mine].astype(F32) + back[a, rows, :].astype(F32)
            back[a, rows, :] = total.astype(BF)

    def send_rows(a):
        add_halves(a, 0)
        for w, way in enumerate(step):
            for n in range(3):
                far[a, w, n] = start(
                    remote(
                        back.at[a, pl.ds(FAR[(way, n)] * CAP, CAP)], distant.at[a, w, n],
                        far_send.at[a, w, n], far_recv.at[a, w, n], far_peer(here, way, n, -1),
                    )
                )
        add_halves(a, 1)
        for i in (3, 4, 1, 2, 0):
            side[a, i] = start(
                remote(
                    back.at[a, pl.ds((5 + i) * CAP, CAP)], beside.at[a, i],
                    side_send.at[a, i], side_recv.at[a, i], here.near(1, 0),
                )
            )

    def spread(a, i, more, out):
        side[a, i].wait_recv()
        meta = metas[i]
        slots = slots_of(here, i)
        if a:
            tables = [plain_table(meta, slots).astype(BF)]
        else:
            exact = gate_table(meta, slots)
            high = exact.astype(BF)
            tables = [high, (exact - high.astype(F32)).astype(BF)]

        @pl.loop(0, HALF // COL)
        def _(c):
            cols = pl.ds(pl.multiple_of(c * COL, COL), COL)
            rows = [back[a, pl.ds(i * CAP, CAP), cols], beside[a, i, :, cols]]
            if i >= 3:
                rows += [distant[a, i - 3, n, :, cols] for n in range(3)]
            rows = jnp.concatenate(rows, axis=0)
            total = None
            for table in tables:
                term = lax.dot_general(table, rows, (((0,), (0,)), ((), ())), preferred_element_type=F32)
                total = term if total is None else total + term
            for ref in more:
                total = total + ref[:, cols].astype(F32)
            out[:, cols] = total.astype(BF)

    def sum_two(a):
        for w in range(2):
            for n in range(3):
                far[a, w, n].wait_recv()
            spread(a, 3 + w, [], comp.at[a, w])
            tree[a, w] = start(
                remote(
                    comp.at[a, w], got_two.at[a, w], tree_send.at[a, w], tree_recv.at[a, w], here.near(0, -step[w])
                )
            )

    def sum_one(a):
        for w in range(2):
            tree[a, w].wait_recv()
            spread(a, 1 + w, [got_two.at[a, w]], comp.at[a, 2 + w])
            tree[a, 2 + w] = start(
                remote(
                    comp.at[a, 2 + w], got_one.at[a, w], tree_send.at[a, 2 + w], tree_recv.at[a, 2 + w],
                    here.near(0, -step[w]),
                )
            )

    def sum_home(a, out):
        for w in range(2):
            tree[a, 2 + w].wait_recv()
        spread(a, 0, [got_one.at[a, 0], got_one.at[a, 1]], out)

    first_hop(0)
    for load in loads[1:]:
        load.start()
    metas[0] = make_meta(routes[...], gates[...], dropped[...], placement)
    about = []
    for i in range(1, 5):
        depth, way = STEPS[i]
        about.append(
            start(remote(metas.at[0], metas.at[i], meta_send.at[i - 1], meta_recv.at[i - 1], here.near(0, way * depth)))
        )
    loads[0].wait()
    pick(0, 0)
    second_hop(0)
    first_hop(1)
    for copy in about:
        copy.wait_recv()
    pick(0, 1)
    pick(0, 2)
    loads[1].wait()
    pick(1, 0)
    pick(0, 3)
    pick(0, 4)
    second_hop(1)
    pick(1, 1)
    pick(1, 2)
    collect(0)
    for load in loads[2:]:
        load.wait()
    whole(0)
    forward(0)
    forward(1)
    pick(1, 3)
    pick(1, 4)
    activate()
    forward_out()
    swap_halves(0)
    collect(1)
    send_rows(0)
    whole(1)
    for i in range(1, 5):
        for a in range(2):
            sent(hop[a, i])
    for n in range(2):
        sent(core[0, n])
    for j in range(16):
        sent(pair[0, j])
    weight_terms((2,), hidden, rows_cot)
    backward_hidden()
    sum_two(0)
    weight_terms((0, 1), slopes, rows_tok)
    ring_step(2)
    sum_one(0)
    backward_rows()
    swap_halves(1)
    ring_step(0)
    send_rows(1)
    ring_step(1)
    sum_two(1)
    sum_home(0, mixed)
    cross_step(2)
    sum_one(1)
    cross_step(0)
    sum_home(1, input_grad)
    last_step(2)
    cross_step(1)
    last_step(0)
    last_step(1)
    for copy in waiting:
        copy.wait_send()


OUTS = ((TOK, HALF), (TOK, HALF), (512, FF), (512, FF), (FF, 512))


def layer(tok, cot, routes, gates, dropped, placement, w_gate, w_up, w_down):
    vmem = pl.BlockSpec(memory_space=pltpu.VMEM)
    hbm = pl.BlockSpec(memory_space=pl.ANY)
    smem = pl.BlockSpec(memory_space=pltpu.SMEM)
    dma = pltpu.SemaphoreType.DMA
    return pl.pallas_call(
        layer_kernel,
        out_shape=tuple(jax.ShapeDtypeStruct(shape, BF) for shape in OUTS),
        in_specs=[hbm, hbm, vmem, vmem, vmem, smem, hbm, hbm, hbm],
        out_specs=(vmem,) * 5,
        scratch_shapes=[
            pltpu.VMEM((TOK, HALF), BF),
            pltpu.VMEM((TOK, HALF), BF),
            pltpu.VMEM((5, 8, TOK), F32),
            pltpu.VMEM((2, 4, TOK, HALF), BF),
            pltpu.VMEM((2, 11, CAP, HALF), BF),
            pltpu.VMEM((ROWS, FULL), BF),
            pltpu.VMEM((ROWS, FULL), BF),
            pltpu.VMEM((FULL, 2 * FF), BF),
            pltpu.VMEM((FF, FULL), BF),
            pltpu.VMEM((ROWS, 2 * FF), F32),
            pltpu.VMEM((ROWS, FF), BF),
            pltpu.VMEM((ROWS, 2 * FF), BF),
            pltpu.VMEM((3 * FF, FULL), BF),
            pltpu.VMEM((2, ROWS, HALF), BF),
            pltpu.VMEM((2, 5, CAP, HALF), BF),
            pltpu.VMEM((2, 2, 3, CAP, HALF), BF),
            pltpu.VMEM((2, 2, TOK, HALF), BF),
            pltpu.VMEM((2, 2, TOK, HALF), BF),
            pltpu.VMEM((3, 2, FF, 512), BF),
            pltpu.VMEM((3, 2, 2, FF, 512), BF),
            pltpu.VMEM((3, FF, 512), BF),
            dma((4,)), dma((4,)),
            dma((2, 4)), dma((2, 4)),
            dma((2, 11)), dma((2, 11)),
            dma((2, 16)), dma((2, 16)),
            dma((2, 2)), dma((2, 2)),
            dma((2, 5)), dma((2, 5)),
            dma((2, 2, 3)), dma((2, 2, 3)),
            dma((2, 4)), dma((2, 4)),
            dma((3, 2)), dma((3, 2)),
            dma((3, 2)), dma((3, 2)),
            dma((3, 2)), dma((3, 2)),
            dma((3,)), dma((3,)),
            dma((5,)),
        ],
        compiler_params=pltpu.CompilerParams(
            collective_id=1, has_side_effects=True, vmem_limit_bytes=63 * MIB
        ),
        name="layer",
    )(tok, cot, routes, gates, dropped, placement, w_gate, w_up, w_down)


def finish_kernel(*refs):
    count = len(OUTS)
    held, load_sem, store_sem = refs[2 * count : 3 * count], refs[3 * count], refs[3 * count + 1]
    loads = [pltpu.make_async_copy(refs[i], held[i], load_sem.at[i]) for i in range(count)]
    stores = [pltpu.make_async_copy(held[i], refs[count + i], store_sem.at[i]) for i in range(count)]
    for load in loads:
        load.start()
    for load, store in zip(loads, stores):
        load.wait()
        store.start()
    for store in stores:
        store.wait()


def finish(*arrays):
    hbm = pl.BlockSpec(memory_space=pl.ANY)
    return pl.pallas_call(
        finish_kernel,
        out_shape=tuple(jax.ShapeDtypeStruct(shape, BF) for shape in OUTS),
        in_specs=[hbm] * len(OUTS),
        out_specs=(hbm,) * len(OUTS),
        scratch_shapes=[pltpu.VMEM(shape, BF) for shape in OUTS]
        + [pltpu.SemaphoreType.DMA((len(OUTS),))] * 2,
        name="finish",
    )(*arrays)


def per_device(tokens, routes, gates, dropped, placement, w_gate, w_up, w_down, cotangent):
    mixed, input_grad, grad_gate, grad_up, grad_down = finish(
        *layer(tokens, cotangent, routes.T, gates.T, dropped.T, placement, w_gate[0], w_up[0], w_down[0])
    )
    return mixed, input_grad, grad_gate[None], grad_up[None], grad_down[None]


def solution(mesh):
    in_specs = (
        P(("dp", "expert"), "tensor"),
        P(("dp", "expert"), None),
        P(("dp", "expert"), None),
        P(("dp", "expert"), None),
        P(),
        P("expert", None, "tensor"),
        P("expert", None, "tensor"),
        P("expert", "tensor", None),
        P(("dp", "expert"), "tensor"),
    )
    out_specs = (
        P(("dp", "expert"), "tensor"),
        P(("dp", "expert"), "tensor"),
        P("expert", "dp", "tensor"),
        P("expert", "dp", "tensor"),
        P("expert", "tensor", "dp"),
    )
    return jax.shard_map(
        per_device, mesh=mesh, in_specs=in_specs, out_specs=out_specs, check_vma=False
    )
```

time: 232 us -> 189 us (0.81)
  matrix products: 32.1 us -> 0 us
  local copies, waits for them, and re-layouts: 12.8 us -> 0 us
  Pallas kernels: 185 us -> 188 us
    dot_general x9 -> x0, matrix products: 32.1 us -> none  [the longest x1 4.36 us: per_device(): up_pre = jnp.dot(rows, up_matrix, preferred_element_type=F32)]
    unnamed x19 -> x0, local copies, waits for them, and re-layouts: 11.9 us -> none
    pallas_call x2, Pallas kernels: 185 us -> 188 us  [the longest x1 186 us: layer(): pl.pallas_call(layer_kernel, out_shape=tuple((jax.ShapeDtypeStruct(shape,...]
where the time goes in v2:
time: 189 us
  Pallas kernels  188 us (99%)
    pallas_call x1, Pallas kernels, layer(): pl.pallas_call(layer_kernel, out_shape=tuple((jax.ShapeDtypeStruct(shape,...  186 us

profile of v2, /device:TPU:1, one launch (start us, length us, event | category | flops | bytes accessed | tf_op | source)
XLA Modules:
  0.0 189.0 jit_solution(15596581400938940229)
XLA Ops:
  0.6 185.8 %layer.1 = (bf16[128,2048]{1,0:T(8,128)(2,1)}, bf16[128,2048]{1,0:T(8,128)(2,1)}, bf16[512,384]{1,0:T(8,128)(2,1)}, bf16[512,384]{1,0:T(8,128)(2,1)}, bf16[384,512]{1,0:T(8,128)(2,1)}) custom-call(bf16[128,2048]{1,0:T(8,128)(2,1)} %tok.1, bf16[128,2048]{1,0:T(8,128)(2,1)} %cot.1, s32[2,128]{1,0:T(2,128)} %bitcast.12, f32[2,128]{1,0:T(2,128)} %bitcast.13, ...), custom_call_target="tpu_custom_call" | custom-call | tf_op jit(solution)/shard_map/layer/pallas_call | solution.py:531
  186.5 2.5 %finish.1 = (bf16[128,2048]{1,0:T(8,128)(2,1)}, bf16[128,2048]{1,0:T(8,128)(2,1)}, bf16[512,384]{1,0:T(8,128)(2,1)}, bf16[512,384]{1,0:T(8,128)(2,1)}, bf16[384,512]{1,0:T(8,128)(2,1)}) custom-call(bf16[128,2048]{1,0:T(8,128)(2,1)} %get-tuple-element.15.refs_0_, bf16[128,2048]{1,0:T(8,128)(2,1)} %get-tuple-element.16.refs_1_, ...), custom_call_target="tpu_custom_call" | custom-call | tf_op jit(solution)/shard_map/finish/pallas_call | solution.py:595

commit v3 on v2

--- a/solution.py
+++ b/solution.py
@@ -42,6 +42,13 @@
 
     def along_y(self, dy):
         return (lax.rem(self.y + dy + 4, 4) * 2 + self.xh, self.slot(0, 0), self.core)
+
+    def twin(self):
+        y = self.y + 1 - 2 * lax.rem(self.y, 2)
+        return (y * 2 + self.xh, self.slot(0, 0), self.core)
+
+    def mate(self):
+        return ((3 - self.y) * 2 + self.xh, self.slot(0, 0), self.core)
 
     def other_xh(self):
         return (self.y * 2 + 1 - self.xh, self.slot(0, 0), self.core)
@@ -136,11 +143,13 @@
 def layer_kernel(
     tok, cot, routes, gates, dropped, placement, w_gate, w_up, w_down,
     mixed, input_grad, sum_gate, sum_up, sum_down,
-    tokv, cotv, metas, comp, sendb, rows_tok, rows_cot, wide, down, pre, hidden, slopes, terms,
-    back, beside, distant, got_two, got_one, first, middle, got,
+    tokv, cotv, metas, comp, sendb, rows_tok, rows_cot, weights, down, pre, hidden, slopes, part_out,
+    twin_tok, twin_slopes, term_wide, term_down,
+    back, beside, distant, got_two, got_one, got_pair, got_wide, first_down, middle_down, got_down,
     meta_send, meta_recv, hop_send, hop_recv, row_send, row_recv, pair_send, pair_recv,
     core_send, core_recv, side_send, side_recv, far_send, far_recv, tree_send, tree_recv,
-    ring_send, ring_recv, plain_send, plain_recv, mid_send, mid_recv, cross_send, cross_recv, load_sem,
+    ring_send, ring_recv, plain_send, plain_recv, mid_send, mid_recv, mate_send, mate_recv,
+    cross_send, cross_recv, twin_send, twin_recv, load_sem,
 ):
     here = Place()
     waiting = []
@@ -157,8 +166,8 @@
     loads = [
         pltpu.make_async_copy(tok, tokv, load_sem.at[0]),
         pltpu.make_async_copy(cot, cotv, load_sem.at[1]),
-        pltpu.make_async_copy(w_gate, wide.at[:, pl.ds(0, FF)], load_sem.at[2]),
-        pltpu.make_async_copy(w_up, wide.at[:, pl.ds(FF, FF)], load_sem.at[3]),
+        pltpu.make_async_copy(w_gate, weights.at[:, pl.ds(0, FF)], load_sem.at[2]),
+        pltpu.make_async_copy(w_up, weights.at[:, pl.ds(FF, FF)], load_sem.at[3]),
         pltpu.make_async_copy(w_down, down, load_sem.at[4]),
     ]
     barrier(tree_peers(here) + [here.along_y(1), here.along_y(-1), here.other_xh()])
@@ -171,26 +180,32 @@
     theirs = pl.ds(pl.multiple_of((1 - here.core) * HALF, HALF), HALF)
     hop, row, pair = {}, {}, {}
 
+    def hop_copy(a, i, h, block):
+        cols = pl.ds(h * 1024, 1024)
+        way = STEPS[i][1]
+        hop[a, i, h] = start(
+            remote(
+                block.at[:, cols], comp.at[a, i - 1, :, cols],
+                hop_send.at[a, i - 1, h], hop_recv.at[a, i - 1, h], here.near(0, way),
+            )
+        )
+
     def first_hop(a):
-        for i in (1, 2):
-            hop[a, i] = start(
-                remote(source[a], comp.at[a, i - 1], hop_send.at[a, i - 1], hop_recv.at[a, i - 1], here.near(0, STEPS[i][1]))
-            )
+        for h in range(2):
+            for i in (1, 2):
+                hop_copy(a, i, h, source[a])
 
     def second_hop(a):
-        for i in (1, 2):
-            hop[a, i].wait_recv()
-            hop[a, i + 2] = start(
-                remote(comp.at[a, i - 1], comp.at[a, i + 1], hop_send.at[a, i + 1], hop_recv.at[a, i + 1], here.near(0, STEPS[i][1]))
-            )
+        for h in range(2):
+            for i in (1, 2):
+                hop[a, i, h].wait_recv()
+                hop_copy(a, i + 2, h, comp.at[a, i - 1])
 
     def to_core(a, j):
         part = final[a].at[pl.ds(j * CAP, CAP), mine]
         pair[a, j] = start(remote(part, part, pair_send.at[a, j], pair_recv.at[a, j], here.other_core()))
 
     def pick(a, i):
-        if i >= 3:
-            hop[a, i].wait_recv()
         block = local[a] if i == 0 else comp.at[a, i - 1]
         meta = metas[i]
         slots = slots_of(here, i)
@@ -198,8 +213,7 @@
         weight = jnp.sum(gate_table(meta, slots), axis=1, keepdims=True) if a else None
         places = [5 + i] + (far_places(i) if i >= 3 else [])
 
-        @pl.loop(0, HALF // COL)
-        def _(c):
+        def select(c):
             cols = pl.ds(pl.multiple_of(c * COL, COL), COL)
             part = jnp.dot(table, block[:, cols], preferred_element_type=F32)
             if a:
@@ -210,8 +224,12 @@
             for n, j in enumerate(places):
                 sendb[a, j - 5, :, cols] = part[(n + 1) * CAP : (n + 2) * CAP]
 
+        for h in range(2):
+            if i >= 3 and (a or h):
+                hop[a, i, h].wait_recv()
+            pl.loop(2 * h, 2 * h + 2)(select)
         way = STEPS[i][1]
-        for j in places[1:] + places[:1]:
+        for j in places[:0:-1] + places[:1]:
             peer = here.near(1, 0) if j < 10 else far_peer(here, way, places.index(j) - 1, 1)
             row[a, j] = start(
                 remote(
@@ -222,7 +240,7 @@
         to_core(a, i)
 
     def collect(a):
-        for j in (5, 6, 7, 8, 9, 10, 11, 12, 13, 14, 15):
+        for j in range(5, 16):
             row[a, j].wait_recv()
             to_core(a, j)
 
@@ -236,7 +254,7 @@
         @pl.loop(0, 3)
         def _(c):
             cols = pl.ds(pl.multiple_of(c * 256, 256), 256)
-            pre[rows, cols] = jnp.dot(rows_tok[rows, :], wide[:, cols], preferred_element_type=F32)
+            pre[rows, cols] = jnp.dot(rows_tok[rows, :], weights[:, cols], preferred_element_type=F32)
 
     def activate():
         @pl.loop(0, ROWS // 64)
@@ -249,7 +267,7 @@
         @pl.loop(0, FULL // 256)
         def _(c):
             cols = pl.ds(pl.multiple_of(c * 256, 256), 256)
-            terms[pl.ds(0, ROWS), cols] = jnp.dot(
+            part_out[:, cols] = jnp.dot(
                 hidden[...], down[:, cols], preferred_element_type=F32
             ).astype(BF)
 
@@ -261,100 +279,150 @@
             gate, up = pre[rows, :FF], pre[rows, FF:]
             sigmoid = jax.nn.sigmoid(gate)
             slope = sigmoid * (1.0 + gate * (1.0 - sigmoid))
-            slopes[rows, :FF] = (grad * up * slope).astype(BF)
-            slopes[rows, FF:] = (grad * (gate * sigmoid)).astype(BF)
+            slopes[0, rows, :] = (grad * up * slope).astype(BF)
+            slopes[1, rows, :] = (grad * (gate * sigmoid)).astype(BF)
 
     def backward_rows():
-        both = slopes[...]
+        both = jnp.concatenate([slopes[0], slopes[1]], axis=1)
 
         @pl.loop(0, FULL // 256)
         def _(c):
             cols = pl.ds(pl.multiple_of(c * 256, 256), 256)
-            rows_tok[:, cols] = lax.dot_general(both, wide[cols, :], NT, preferred_element_type=F32).astype(BF)
-
+            rows_cot[:, cols] = lax.dot_general(both, weights[cols, :], NT, preferred_element_type=F32).astype(BF)
+
+    low = lax.div(here.y * (3 - here.y), 2)
+    home_part = lax.div(here.y, 2)
     chunk_of = [lax.rem(here.y + 1, 4), lax.rem(here.y + 3, 4)]
     opposite = lax.rem(here.y + 2, 4)
+    away = 1 - here.xh
     step = (1, -1)
-    sums = (sum_gate, sum_up, sum_down)
-    ring, plain, mid, cross = {}, {}, {}, {}
-
-    def share(p, chunk, half):
-        return terms.at[pl.ds(p * FF, FF), pl.ds(pl.multiple_of(chunk * 1024 + half * 512, 512), 512)]
-
-    def weight_terms(pieces, small, big):
-        at, size = pieces[0] * FF, len(pieces) * FF
-        turned = small[...].T
-
-        def chunk_terms(chunk):
-            @pl.loop(0, 4)
-            def _(c):
-                cols = pl.ds(pl.multiple_of(chunk * 1024 + c * 256, 256), 256)
-                terms[pl.ds(at, size), cols] = jnp.dot(turned, big[:, cols], preferred_element_type=F32).astype(BF)
-
-        chunk_terms(opposite)
-        for p in pieces:
-            for w in range(2):
-                ring[p, w] = start(
-                    remote(
-                        share(p, opposite, w), first.at[p, w],
-                        ring_send.at[p, w], ring_recv.at[p, w], here.along_y(step[w]),
-                    )
-                )
-        chunk_terms(chunk_of[0])
-        chunk_terms(chunk_of[1])
-        for p in pieces:
-            for w in range(2):
-                plain[p, w] = start(
-                    remote(
-                        share(p, chunk_of[w], 1 - w), middle.at[p, w, 1 - w],
-                        plain_send.at[p, w], plain_recv.at[p, w], here.along_y(step[w]),
-                    )
-                )
-        chunk_terms(here.y)
+    sums = (sum_gate, sum_up)
+    ring, plain, mid, mate, cross, twin = {}, {}, {}, {}, {}, {}
 
     def by_rows(body, height=64):
         @pl.loop(0, FF // height)
         def _(r):
             body(pl.ds(pl.multiple_of(r * height, height), height))
 
-    def ring_step(p):
+    def part_cols(q):
+        return pl.multiple_of((low + q * (3 - 2 * low)) * 1024, 1024)
+
+    def wide(p, q, h):
+        return term_wide.at[pl.ds(p * FF, FF), pl.ds(pl.multiple_of(q * 1024 + h * 512, 512), 512)]
+
+    def send_twin_rows():
+        chunk = 1 - low + here.core * (1 + 2 * low)
+        twin[0] = start(
+            remote(
+                rows_tok.at[:, pl.ds(pl.multiple_of(chunk * 1024, 1024), 1024)],
+                twin_tok.at[:, pl.ds(pl.multiple_of(here.core * 1024, 1024), 1024)],
+                twin_send.at[0], twin_recv.at[0], here.twin(),
+            )
+        )
+
+    def pass_twin_rows():
+        twin[0].wait_recv()
+        part = twin_tok.at[:, pl.ds(pl.multiple_of(here.core * 1024, 1024), 1024)]
+        twin[1] = start(remote(part, part, twin_send.at[1], twin_recv.at[1], here.other_core()))
+
+    def send_twin_slopes():
+        for p in range(2):
+            twin[2 + p] = start(
+                remote(slopes.at[p], twin_slopes.at[p], twin_send.at[2 + p], twin_recv.at[2 + p], here.twin())
+            )
+
+    def wide_terms(p, q, small, twin_small):
+        @pl.loop(0, 4)
+        def _(c):
+            cols = pl.ds(pl.multiple_of(part_cols(q) + c * 256, 256), 256)
+            at = pl.ds(pl.multiple_of(q * 1024 + c * 256, 256), 256)
+            total = jnp.dot(small, rows_tok[:, cols], preferred_element_type=F32)
+            total = total + jnp.dot(twin_small, twin_tok[:, at], preferred_element_type=F32)
+            term_wide[pl.ds(p * FF, FF), at] = total.astype(BF)
+
+    def send_mate(p):
+        for h in range(2):
+            mate[p, h] = start(
+                remote(wide(p, 1 - home_part, h), got_pair.at[p, h], mate_send.at[p, h], mate_recv.at[p, h], here.mate())
+            )
+
+    def cross_wide(p):
+        for h in range(2):
+            mate[p, h].wait_recv()
+        a, b = wide(p, home_part, away), got_pair.at[p, away]
+
+        def body(r):
+            a[r, :] = (a[r, :].astype(F32) + b[r, :].astype(F32)).astype(BF)
+
+        by_rows(body)
+        cross[p] = start(remote(a, got_wide.at[p], cross_send.at[p], cross_recv.at[p], here.other_xh()))
+
+    def last_wide(p):
+        cross[p].wait_recv()
+        a, b, c = wide(p, home_part, here.xh), got_pair.at[p, here.xh], got_wide.at[p]
+        for n in range(3):
+            r = pl.ds(n * 128, 128)
+            total = a[r, :].astype(F32) + b[r, :].astype(F32) + c[r, :].astype(F32)
+            sums[p][:, r] = total.T.astype(BF)
+
+    def share(chunk, half):
+        return term_down.at[:, pl.ds(pl.multiple_of(chunk * 1024 + half * 512, 512), 512)]
+
+    def down_terms(turned, chunk):
+        @pl.loop(0, 4)
+        def _(c):
+            cols = pl.ds(pl.multiple_of(chunk * 1024 + c * 256, 256), 256)
+            term_down[:, cols] = jnp.dot(turned, rows_cot[:, cols], preferred_element_type=F32).astype(BF)
+
+    def send_ring():
         for w in range(2):
-            ring[p, w].wait_recv()
-            a, b = share(p, chunk_of[w], w), first.at[p, w]
+            ring[w] = start(
+                remote(share(opposite, w), first_down.at[w], ring_send.at[w], ring_recv.at[w], here.along_y(step[w]))
+            )
+
+    def send_plain():
+        for w in range(2):
+            plain[w] = start(
+                remote(
+                    share(chunk_of[w], 1 - w), middle_down.at[w, 1 - w],
+                    plain_send.at[w], plain_recv.at[w], here.along_y(step[w]),
+                )
+            )
+
+    def ring_step():
+        for w in range(2):
+            ring[w].wait_recv()
+            a, b = share(chunk_of[w], w), first_down.at[w]
 
             def body(r, a=a, b=b):
                 a[r, :] = (a[r, :].astype(F32) + b[r, :].astype(F32)).astype(BF)
 
             by_rows(body)
-            mid[p, w] = start(
-                remote(a, middle.at[p, w, w], mid_send.at[p, w], mid_recv.at[p, w], here.along_y(step[w]))
-            )
-
-    def cross_step(p):
+            mid[w] = start(remote(a, middle_down.at[w, w], mid_send.at[w], mid_recv.at[w], here.along_y(step[w])))
+
+    def cross_down():
         for w in range(2):
-            plain[p, w].wait_recv()
-            mid[p, w].wait_recv()
-        away = 1 - here.xh
-        a, b, c = share(p, here.y, away), middle.at[p, 0, away], middle.at[p, 1, away]
+            plain[w].wait_recv()
+            mid[w].wait_recv()
+        a, b, c = share(here.y, away), middle_down.at[0, away], middle_down.at[1, away]
 
         def body(r):
             a[r, :] = (a[r, :].astype(F32) + b[r, :].astype(F32) + c[r, :].astype(F32)).astype(BF)
 
         by_rows(body)
-        cross[p] = start(remote(a, got.at[p], cross_send.at[p], cross_recv.at[p], here.other_xh()))
-
-    def last_step(p):
-        cross[p].wait_recv()
-        a, b, c = share(p, here.y, here.xh), middle.at[p, 0, here.xh], middle.at[p, 1, here.xh]
-        for n in range(3):
-            r = pl.ds(n * 128, 128)
-            total = a[r, :].astype(F32) + b[r, :].astype(F32) + c[r, :].astype(F32) + got[p, r, :].astype(F32)
-            if p == 2:
-                sums[p][r, :] = total.astype(BF)
-            else:
-                sums[p][:, r] = total.T.astype(BF)
-
-    parts = (terms, rows_tok)
+        cross[2] = start(remote(a, got_down, cross_send.at[2], cross_recv.at[2], here.other_xh()))
+
+    def last_down():
+        cross[2].wait_recv()
+        a, b, c = share(here.y, here.xh), middle_down.at[0, here.xh], middle_down.at[1, here.xh]
+
+        def body(r):
+            total = a[r, :].astype(F32) + b[r, :].astype(F32) + c[r, :].astype(F32) + got_down[r, :].astype(F32)
+            sum_down[r, :] = total.astype(BF)
+
+        by_rows(body)
+
+    parts = (part_out, rows_cot)
     spans = ((10 * CAP, 6 * CAP), (0, 10 * CAP))
     core, side, far, tree = {}, {}, {}, {}
 
@@ -462,19 +530,23 @@
     loads[0].wait()
     pick(0, 0)
     second_hop(0)
-    first_hop(1)
     for copy in about:
         copy.wait_recv()
     pick(0, 1)
     pick(0, 2)
     loads[1].wait()
     pick(1, 0)
+    early = [hop[0, i, 0] for i in (3, 4)]
+    for copy in early:
+        copy.wait_recv()
+    first_hop(1)
     pick(0, 3)
     pick(0, 4)
     second_hop(1)
     pick(1, 1)
     pick(1, 2)
     collect(0)
+    send_twin_rows()
     for load in loads[2:]:
         load.wait()
     whole(0)
@@ -485,37 +557,51 @@
     activate()
     forward_out()
     swap_halves(0)
+    pass_twin_rows()
     collect(1)
     send_rows(0)
+    hidden_turned = hidden[...].T
     whole(1)
+    down_terms(hidden_turned, opposite)
+    send_ring()
+    backward_hidden()
+    send_twin_slopes()
+    down_terms(hidden_turned, chunk_of[0])
+    down_terms(hidden_turned, chunk_of[1])
+    send_plain()
     for i in range(1, 5):
         for a in range(2):
-            sent(hop[a, i])
-    for n in range(2):
-        sent(core[0, n])
+            for h in range(2):
+                sent(hop[a, i, h])
+    sum_two(0)
+    ring_step()
+    down_terms(hidden_turned, here.y)
     for j in range(16):
-        sent(pair[0, j])
-    weight_terms((2,), hidden, rows_cot)
-    backward_hidden()
-    sum_two(0)
-    weight_terms((0, 1), slopes, rows_tok)
-    ring_step(2)
-    sum_one(0)
+        sent(pair[1, j])
     backward_rows()
     swap_halves(1)
-    ring_step(0)
+    sum_one(0)
     send_rows(1)
-    ring_step(1)
+    turned = [slopes[p].T for p in range(2)]
+    twin[1].wait_recv()
+    twin_turned = []
+    for p in range(2):
+        twin[2 + p].wait_recv()
+        twin_turned.append(twin_slopes[p].T)
+        wide_terms(p, 1 - home_part, turned[p], twin_turned[p])
+        send_mate(p)
     sum_two(1)
+    for p in range(2):
+        wide_terms(p, home_part, turned[p], twin_turned[p])
+    cross_down()
+    sum_one(1)
+    cross_wide(0)
     sum_home(0, mixed)
-    cross_step(2)
-    sum_one(1)
-    cross_step(0)
+    cross_wide(1)
+    last_down()
+    last_wide(0)
     sum_home(1, input_grad)
-    last_step(2)
-    cross_step(1)
-    last_step(0)
-    last_step(1)
+    last_wide(1)
     for copy in waiting:
         copy.wait_send()
 
@@ -545,28 +631,36 @@
             pltpu.VMEM((FF, FULL), BF),
             pltpu.VMEM((ROWS, 2 * FF), F32),
             pltpu.VMEM((ROWS, FF), BF),
-            pltpu.VMEM((ROWS, 2 * FF), BF),
-            pltpu.VMEM((3 * FF, FULL), BF),
+            pltpu.VMEM((2, ROWS, FF), BF),
+            pltpu.VMEM((ROWS, FULL), BF),
+            pltpu.VMEM((ROWS, HALF), BF),
+            pltpu.VMEM((2, ROWS, FF), BF),
+            pltpu.VMEM((2 * FF, HALF), BF),
+            pltpu.VMEM((FF, FULL), BF),
             pltpu.VMEM((2, ROWS, HALF), BF),
             pltpu.VMEM((2, 5, CAP, HALF), BF),
             pltpu.VMEM((2, 2, 3, CAP, HALF), BF),
             pltpu.VMEM((2, 2, TOK, HALF), BF),
             pltpu.VMEM((2, 2, TOK, HALF), BF),
-            pltpu.VMEM((3, 2, FF, 512), BF),
-            pltpu.VMEM((3, 2, 2, FF, 512), BF),
-            pltpu.VMEM((3, FF, 512), BF),
+            pltpu.VMEM((2, 2, FF, 512), BF),
+            pltpu.VMEM((2, FF, 512), BF),
+            pltpu.VMEM((2, FF, 512), BF),
+            pltpu.VMEM((2, 2, FF, 512), BF),
+            pltpu.VMEM((FF, 512), BF),
             dma((4,)), dma((4,)),
-            dma((2, 4)), dma((2, 4)),
+            dma((2, 4, 2)), dma((2, 4, 2)),
             dma((2, 11)), dma((2, 11)),
             dma((2, 16)), dma((2, 16)),
             dma((2, 2)), dma((2, 2)),
             dma((2, 5)), dma((2, 5)),
             dma((2, 2, 3)), dma((2, 2, 3)),
             dma((2, 4)), dma((2, 4)),
-            dma((3, 2)), dma((3, 2)),
-            dma((3, 2)), dma((3, 2)),
-            dma((3, 2)), dma((3, 2)),
+            dma((2,)), dma((2,)),
+            dma((2,)), dma((2,)),
+            dma((2,)), dma((2,)),
+            dma((2, 2)), dma((2, 2)),
             dma((3,)), dma((3,)),
+            dma((4,)), dma((4,)),
             dma((5,)),
         ],
         compiler_params=pltpu.CompilerParams(

time: 189 us -> 175 us (0.926)
  Pallas kernels: 188 us -> 173 us
    pallas_call x1, Pallas kernels: 186 us -> 171 us  [layer(): pl.pallas_call(layer_kernel, out_shape=tuple((jax.ShapeDtypeStruct(shape,...]
where the time goes in v3:
time: 175 us; the launch traced here: 174 us
  Pallas kernels  173 us (99%)
    pallas_call x1, Pallas kernels, layer(): pl.pallas_call(layer_kernel, out_shape=tuple((jax.ShapeDtypeStruct(shape,...  171 us

profile of v3, /device:TPU:1, one launch (start us, length us, event | category | flops | bytes accessed | tf_op | source)
XLA Modules:
  0.0 174.0 jit_solution(16511450621507849274)
XLA Ops:
  0.6 170.9 %layer.1 = (bf16[128,2048]{1,0:T(8,128)(2,1)}, bf16[128,2048]{1,0:T(8,128)(2,1)}, bf16[512,384]{1,0:T(8,128)(2,1)}, bf16[512,384]{1,0:T(8,128)(2,1)}, bf16[384,512]{1,0:T(8,128)(2,1)}) custom-call(bf16[128,2048]{1,0:T(8,128)(2,1)} %tok.1, bf16[128,2048]{1,0:T(8,128)(2,1)} %cot.1, s32[2,128]{1,0:T(2,128)} %bitcast.12, f32[2,128]{1,0:T(2,128)} %bitcast.13, ...), custom_call_target="tpu_custom_call" | custom-call | tf_op jit(solution)/shard_map/layer/pallas_call | solution.py:617
  171.5 2.5 %finish.1 = (bf16[128,2048]{1,0:T(8,128)(2,1)}, bf16[128,2048]{1,0:T(8,128)(2,1)}, bf16[512,384]{1,0:T(8,128)(2,1)}, bf16[512,384]{1,0:T(8,128)(2,1)}, bf16[384,512]{1,0:T(8,128)(2,1)}) custom-call(bf16[128,2048]{1,0:T(8,128)(2,1)} %get-tuple-element.15.refs_0_, bf16[128,2048]{1,0:T(8,128)(2,1)} %get-tuple-element.16.refs_1_, ...), custom_call_target="tpu_custom_call" | custom-call | tf_op jit(solution)/shard_map/finish/pallas_call | solution.py:689

commit v4 on v3

--- a/solution.py
+++ b/solution.py
@@ -340,15 +340,18 @@
             total = total + jnp.dot(twin_small, twin_tok[:, at], preferred_element_type=F32)
             term_wide[pl.ds(p * FF, FF), at] = total.astype(BF)
 
-    def send_mate(p):
-        for h in range(2):
-            mate[p, h] = start(
-                remote(wide(p, 1 - home_part, h), got_pair.at[p, h], mate_send.at[p, h], mate_recv.at[p, h], here.mate())
-            )
+    half_of = (away, here.xh)
+
+    def send_mate(p, n):
+        mate[p, n] = start(
+            remote(
+                wide(p, 1 - home_part, half_of[n]), got_pair.at[p, half_of[n]],
+                mate_send.at[p, n], mate_recv.at[p, n], here.mate(),
+            )
+        )
 
     def cross_wide(p):
-        for h in range(2):
-            mate[p, h].wait_recv()
+        mate[p, 0].wait_recv()
         a, b = wide(p, home_part, away), got_pair.at[p, away]
 
         def body(r):
@@ -358,6 +361,7 @@
         cross[p] = start(remote(a, got_wide.at[p], cross_send.at[p], cross_recv.at[p], here.other_xh()))
 
     def last_wide(p):
+        mate[p, 1].wait_recv()
         cross[p].wait_recv()
         a, b, c = wide(p, home_part, here.xh), got_pair.at[p, here.xh], got_wide.at[p]
         for n in range(3):
@@ -557,7 +561,6 @@
     activate()
     forward_out()
     swap_halves(0)
-    pass_twin_rows()
     collect(1)
     send_rows(0)
     hidden_turned = hidden[...].T
@@ -566,6 +569,7 @@
     send_ring()
     backward_hidden()
     send_twin_slopes()
+    pass_twin_rows()
     down_terms(hidden_turned, chunk_of[0])
     down_terms(hidden_turned, chunk_of[1])
     send_plain()
@@ -589,19 +593,21 @@
         twin[2 + p].wait_recv()
         twin_turned.append(twin_slopes[p].T)
         wide_terms(p, 1 - home_part, turned[p], twin_turned[p])
-        send_mate(p)
-    sum_two(1)
+        send_mate(p, 0)
+    for p in range(2):
+        send_mate(p, 1)
     for p in range(2):
         wide_terms(p, home_part, turned[p], twin_turned[p])
+    sum_two(1)
+    cross_wide(0)
+    cross_wide(1)
+    sum_home(0, mixed)
+    sum_one(1)
     cross_down()
-    sum_one(1)
-    cross_wide(0)
-    sum_home(0, mixed)
-    cross_wide(1)
     last_down()
     last_wide(0)
+    last_wide(1)
     sum_home(1, input_grad)
-    last_wide(1)
     for copy in waiting:
         copy.wait_send()
 

time: 175 us -> 173 us (0.989); the launches traced: 174 us -> 170 us
  Pallas kernels: 173 us -> 169 us
    pallas_call x1, Pallas kernels: 171 us -> 167 us  [layer(): pl.pallas_call(layer_kernel, out_shape=tuple((jax.ShapeDtypeStruct(shape,...]
where the time goes in v4:
time: 173 us; the launch traced here: 170 us
  Pallas kernels  169 us (98%)
    pallas_call x1, Pallas kernels, layer(): pl.pallas_call(layer_kernel, out_shape=tuple((jax.ShapeDtypeStruct(shape,...  167 us

profile of v4, /device:TPU:1, one launch (start us, length us, event | category | flops | bytes accessed | tf_op | source)
XLA Modules:
  0.0 169.7 jit_solution(14079241654868211643)
XLA Ops:
  0.6 166.5 %layer.1 = (bf16[128,2048]{1,0:T(8,128)(2,1)}, bf16[128,2048]{1,0:T(8,128)(2,1)}, bf16[512,384]{1,0:T(8,128)(2,1)}, bf16[512,384]{1,0:T(8,128)(2,1)}, bf16[384,512]{1,0:T(8,128)(2,1)}) custom-call(bf16[128,2048]{1,0:T(8,128)(2,1)} %tok.1, bf16[128,2048]{1,0:T(8,128)(2,1)} %cot.1, s32[2,128]{1,0:T(2,128)} %bitcast.12, f32[2,128]{1,0:T(2,128)} %bitcast.13, ...), custom_call_target="tpu_custom_call" | custom-call | tf_op jit(solution)/shard_map/layer/pallas_call | solution.py:623
  167.2 2.5 %finish.1 = (bf16[128,2048]{1,0:T(8,128)(2,1)}, bf16[128,2048]{1,0:T(8,128)(2,1)}, bf16[512,384]{1,0:T(8,128)(2,1)}, bf16[512,384]{1,0:T(8,128)(2,1)}, bf16[384,512]{1,0:T(8,128)(2,1)}) custom-call(bf16[128,2048]{1,0:T(8,128)(2,1)} %get-tuple-element.15.refs_0_, bf16[128,2048]{1,0:T(8,128)(2,1)} %get-tuple-element.16.refs_1_, ...), custom_call_target="tpu_custom_call" | custom-call | tf_op jit(solution)/shard_map/finish/pallas_call | solution.py:695

commit v5 on v4

--- a/solution.py
+++ b/solution.py
@@ -54,10 +54,11 @@
         return (self.y * 2 + 1 - self.xh, self.slot(0, 0), self.core)
 
 
-def barrier(peers):
+def barrier(peers, meanwhile):
     sem = pltpu.get_barrier_semaphore()
     for peer in peers:
         pl.semaphore_signal(sem, inc=1, device_id=peer, device_id_type=MESH)
+    meanwhile()
     pl.semaphore_wait(sem, len(peers))
 
 
@@ -170,8 +171,13 @@
         pltpu.make_async_copy(w_up, weights.at[:, pl.ds(FF, FF)], load_sem.at[3]),
         pltpu.make_async_copy(w_down, down, load_sem.at[4]),
     ]
-    barrier(tree_peers(here) + [here.along_y(1), here.along_y(-1), here.other_xh()])
-    loads[0].start()
+
+    def prepare():
+        for load in loads:
+            load.start()
+        metas[0] = make_meta(routes[...], gates[...], dropped[...], placement)
+
+    barrier(tree_peers(here) + [here.along_y(1), here.along_y(-1), here.other_xh()], prepare)
 
     source = (tok, cot)
     local = (tokv, cotv)
@@ -522,9 +528,6 @@
         spread(a, 0, [got_one.at[a, 0], got_one.at[a, 1]], out)
 
     first_hop(0)
-    for load in loads[1:]:
-        load.start()
-    metas[0] = make_meta(routes[...], gates[...], dropped[...], placement)
     about = []
     for i in range(1, 5):
         depth, way = STEPS[i]

time: 173 us -> 173 us (level)
  no operation moved by 1% of the time
where the time goes in v5:
time: 173 us; the launch traced here: 170 us
  Pallas kernels  169 us (98%)
    pallas_call x1, Pallas kernels, layer(): pl.pallas_call(layer_kernel, out_shape=tuple((jax.ShapeDtypeStruct(shape,...  167 us

profile of v5, /device:TPU:1, one launch (start us, length us, event | category | flops | bytes accessed | tf_op | source)
XLA Modules:
  0.0 169.7 jit_solution(2496074514101047795)
XLA Ops:
  0.6 166.6 %layer.1 = (bf16[128,2048]{1,0:T(8,128)(2,1)}, bf16[128,2048]{1,0:T(8,128)(2,1)}, bf16[512,384]{1,0:T(8,128)(2,1)}, bf16[512,384]{1,0:T(8,128)(2,1)}, bf16[384,512]{1,0:T(8,128)(2,1)}) custom-call(bf16[128,2048]{1,0:T(8,128)(2,1)} %tok.1, bf16[128,2048]{1,0:T(8,128)(2,1)} %cot.1, s32[2,128]{1,0:T(2,128)} %bitcast.12, f32[2,128]{1,0:T(2,128)} %bitcast.13, ...), custom_call_target="tpu_custom_call" | custom-call | tf_op jit(solution)/shard_map/layer/pallas_call | solution.py:626
  167.2 2.5 %finish.1 = (bf16[128,2048]{1,0:T(8,128)(2,1)}, bf16[128,2048]{1,0:T(8,128)(2,1)}, bf16[512,384]{1,0:T(8,128)(2,1)}, bf16[512,384]{1,0:T(8,128)(2,1)}, bf16[384,512]{1,0:T(8,128)(2,1)}) custom-call(bf16[128,2048]{1,0:T(8,128)(2,1)} %get-tuple-element.15.refs_0_, bf16[128,2048]{1,0:T(8,128)(2,1)} %get-tuple-element.16.refs_1_, ...), custom_call_target="tpu_custom_call" | custom-call | tf_op jit(solution)/shard_map/finish/pallas_call | solution.py:698
